TPU v7x, 128 devices: a whole 4x4x4 slice. The times are simulated.
128 devices in a mesh: dp: 2 (over y_hi), heads: 32 (over x, z, y_lo), tensor: 2 (over core).
Axes of the slice: x: 4, y: 4 (y_hi: 2, y_lo: 2; y = y_hi * 2 + y_lo), z: 4, core: 2. Of those that a mesh axis runs over, the one named last changes fastest.
Arguments:
- tokens: bfloat16 [2, 4096, 2048], P('dp', 'heads'), may hold values from -6 to 6
- segments: int32 [2, 4096], P('dp', 'heads'), may hold values from 0 to 9, never falling along the last dimension, each value on 1 to 2048 neighbouring positions
- cotangent: bfloat16 [2, 4096, 2048], P('dp', 'heads'), may hold values from -6 to 6
- query_weight: float32 [2048, 2048], P(('dp', 'heads'), 'tensor'), may hold values from -0.125 to 0.125
- key_weight: float32 [2048, 512], P(('dp', 'heads'), 'tensor'), may hold values from -0.125 to 0.125
- value_weight: float32 [2048, 512], P(('dp', 'heads'), 'tensor'), may hold values from -0.125 to 0.125
- output_weight: float32 [2048, 2048], P('tensor', ('dp', 'heads')), may hold values from -0.375 to 0.375
- gate_weight: float32 [2048, 8192], P(('dp', 'heads'), 'tensor'), may hold values from -0.125 to 0.125
- up_weight: float32 [2048, 8192], P(('dp', 'heads'), 'tensor'), may hold values from -0.125 to 0.125
- down_weight: float32 [8192, 2048], P('tensor', ('dp', 'heads')), may hold values from -0.0625 to 0.0625
- norm_gain_pair: float32 [2, 2048], P(None, ('dp', 'heads')), may hold values from 0.5 to 1.5
- query_first: float32 [2048, 2048], P(('dp', 'heads'), 'tensor'), may hold values from -64 to 64
- key_first: float32 [2048, 512], P(('dp', 'heads'), 'tensor'), may hold values from -64 to 64
- value_first: float32 [2048, 512], P(('dp', 'heads'), 'tensor'), may hold values from -64 to 64
- output_first: float32 [2048, 2048], P('tensor', ('dp', 'heads')), may hold values from -16 to 16
- gate_first: float32 [2048, 8192], P(('dp', 'heads'), 'tensor'), may hold values from -16 to 16
- up_first: float32 [2048, 8192], P(('dp', 'heads'), 'tensor'), may hold values from -16 to 16
- down_first: float32 [8192, 2048], P('tensor', ('dp', 'heads')), may hold values from -32 to 32
- gains_first: float32 [2, 2048], P(None, ('dp', 'heads')), may hold values from -48 to 48
- query_second: float32 [2048, 2048], P(('dp', 'heads'), 'tensor'), may hold values from 212.992 to 3440.64
- key_second: float32 [2048, 512], P(('dp', 'heads'), 'tensor'), may hold values from 212.992 to 3440.64
- value_second: float32 [2048, 512], P(('dp', 'heads'), 'tensor'), may hold values from 212.992 to 3440.64
- output_second: float32 [2048, 2048], P('tensor', ('dp', 'heads')), may hold values from 18.8416 to 311.296
- gate_second: float32 [2048, 8192], P(('dp', 'heads'), 'tensor'), may hold values from 18.8416 to 311.296
- up_second: float32 [2048, 8192], P(('dp', 'heads'), 'tensor'), may hold values from 18.8416 to 311.296
- down_second: float32 [8192, 2048], P('tensor', ('dp', 'heads')), may hold values from 77.0048 to 1236.992
- gains_second: float32 [2, 2048], P(None, ('dp', 'heads')), may hold values from 135.9872 to 2203.648
Outputs:
- block_out: bfloat16 [2, 4096, 2048], P('dp', 'heads')
- input_grad: float32 [2, 4096, 2048], P('dp', 'heads')
- query_grad: float32 [2048, 2048], P(('dp', 'heads'), 'tensor')
- query_first_new: float32 [2048, 2048], P(('dp', 'heads'), 'tensor')
- query_second_new: float32 [2048, 2048], P(('dp', 'heads'), 'tensor')
- query_new: float32 [2048, 2048], P(('dp', 'heads'), 'tensor')
- key_grad: float32 [2048, 512], P(('dp', 'heads'), 'tensor')
- key_first_new: float32 [2048, 512], P(('dp', 'heads'), 'tensor')
- key_second_new: float32 [2048, 512], P(('dp', 'heads'), 'tensor')
- key_new: float32 [2048, 512], P(('dp', 'heads'), 'tensor')
- value_grad: float32 [2048, 512], P(('dp', 'heads'), 'tensor')
- value_first_new: float32 [2048, 512], P(('dp', 'heads'), 'tensor')
- value_second_new: float32 [2048, 512], P(('dp', 'heads'), 'tensor')
- value_new: float32 [2048, 512], P(('dp', 'heads'), 'tensor')
- output_grad: float32 [2048, 2048], P('tensor', ('dp', 'heads'))
- output_first_new: float32 [2048, 2048], P('tensor', ('dp', 'heads'))
- output_second_new: float32 [2048, 2048], P('tensor', ('dp', 'heads'))
- output_new: float32 [2048, 2048], P('tensor', ('dp', 'heads'))
- gate_grad: float32 [2048, 8192], P(('dp', 'heads'), 'tensor')
- gate_first_new: float32 [2048, 8192], P(('dp', 'heads'), 'tensor')
- gate_second_new: float32 [2048, 8192], P(('dp', 'heads'), 'tensor')
- gate_new: float32 [2048, 8192], P(('dp', 'heads'), 'tensor')
- up_grad: float32 [2048, 8192], P(('dp', 'heads'), 'tensor')
- up_first_new: float32 [2048, 8192], P(('dp', 'heads'), 'tensor')
- up_second_new: float32 [2048, 8192], P(('dp', 'heads'), 'tensor')
- up_new: float32 [2048, 8192], P(('dp', 'heads'), 'tensor')
- down_grad: float32 [8192, 2048], P('tensor', ('dp', 'heads'))
- down_first_new: float32 [8192, 2048], P('tensor', ('dp', 'heads'))
- down_second_new: float32 [8192, 2048], P('tensor', ('dp', 'heads'))
- down_new: float32 [8192, 2048], P('tensor', ('dp', 'heads'))
- gains_grad: float32 [2, 2048], P(None, ('dp', 'heads'))
- gains_first_new: float32 [2, 2048], P(None, ('dp', 'heads'))
- gains_second_new: float32 [2, 2048], P(None, ('dp', 'heads'))
- gains_new: float32 [2, 2048], P(None, ('dp', 'heads'))
Inputs may be any that keep to these rules, and one draw needn't show every extreme that they name: `segments`: along each sequence the numbers never fall; each document holds 1 to 2048 tokens and one holds exactly 2048.
All inputs are finite; a program needn't handle non-finite values.
Results may differ from a plain program's by a relative error of at most 0.015.
Values may be sent and summed in bfloat16 or wider, within the bound.
A program may use at most 320 MiB of HBM per device.

v0:
```python
import math

import jax
import jax.numpy as jnp
from jax import lax
from jax.sharding import PartitionSpec as P

D = 2048
FF = 8192
HEADS = 32
KV_HEADS = 8
HEAD_DIM = 64
STEP = 10


EPS = 1e-05


def rope_frequency():
    half_size = HEAD_DIM // 2
    base_freq = 500000.0 ** (-(jnp.arange(half_size, dtype=jnp.float32) * 2.0 / HEAD_DIM))
    wavelength = 2.0 * math.pi / base_freq
    smooth = (8192.0 / wavelength - 1.0) / 3.0
    blended = (1.0 - smooth) * base_freq / 32.0 + smooth * base_freq
    return jnp.where(
        wavelength < 2048.0, base_freq, jnp.where(wavelength > 8192.0, base_freq / 32.0, blended)
    )


def rotary_tables(positions):
    frequency = rope_frequency()
    angles = positions.astype(jnp.float32)[:, None] * frequency[None, :]
    return (jnp.cos(angles), jnp.sin(angles))


def rotate(values, cos_tab, sin_tab):
    half_size = values.shape[-1] // 2
    front_part = values[..., :half_size]
    back_part = values[..., half_size:]
    cos_wide = cos_tab[:, None, :]
    sin_wide = sin_tab[:, None, :]
    return jnp.concatenate(
        [
            front_part * cos_wide - back_part * sin_wide,
            back_part * cos_wide + front_part * sin_wide,
        ],
        axis=-1,
    )


def unrotate(values, cos_tab, sin_tab):
    half_size = values.shape[-1] // 2
    front_part = values[..., :half_size]
    back_part = values[..., half_size:]
    cos_wide = cos_tab[:, None, :]
    sin_wide = sin_tab[:, None, :]
    return jnp.concatenate(
        [
            front_part * cos_wide + back_part * sin_wide,
            back_part * cos_wide - front_part * sin_wide,
        ],
        axis=-1,
    )


def contract_last(left, right):
    return lax.dot_general(
        left, right, (((1,), (1,)), ((), ())), preferred_element_type=jnp.float32
    )


def contract_leading_axis(left, right):
    return lax.dot_general(
        left, right, (((0,), (0,)), ((), ())), preferred_element_type=jnp.float32
    )


def folded_normalized(unit_rows, gain_portion, weight_portion):
    gain_fragment = lax.all_gather(gain_portion, ("dp", "heads"), axis=0, tiled=True)
    weight_piece = lax.all_gather(weight_portion, ("dp", "heads"), axis=0, tiled=True)
    normalized_rows = (unit_rows * gain_fragment.astype(jnp.float32)[None, :]).astype(jnp.bfloat16)
    total_sum = jnp.dot(normalized_rows, weight_piece, preferred_element_type=jnp.float32)
    gain_all = gain_fragment.astype(jnp.float32)
    return (total_sum, normalized_rows, gain_all)


def project_out(hidden, weight_portion):
    return jnp.dot(
        hidden,
        lax.all_gather(weight_portion, ("dp", "heads"), axis=1, tiled=True),
        preferred_element_type=jnp.float32,
    )


def project_back(gradient_reduced, weight_portion):
    return contract_last(
        gradient_reduced, lax.all_gather(weight_portion, ("dp", "heads"), axis=1, tiled=True)
    )


def normed_back(gradient_reduced, weight_portion):
    return contract_last(
        gradient_reduced, lax.all_gather(weight_portion, ("dp", "heads"), axis=0, tiled=True)
    )


def input_summands(normalized_every, gradient_reduced, normalized_gradient, unit_rows):
    return (
        contract_leading_axis(normalized_every, gradient_reduced),
        jnp.sum(normalized_gradient * unit_rows, axis=0),
    )


def output_term(gradient_reduced, hidden):
    return contract_leading_axis(gradient_reduced, hidden)


def every_grad(attn_pack, mlp_pack, down_pack, out_pack):
    attn_w, attn_g = input_summands(attn_pack[0], attn_pack[1], attn_pack[2], attn_pack[3])
    mlp_w, mlp_g = input_summands(mlp_pack[0], mlp_pack[1], mlp_pack[2], mlp_pack[3])
    down_term = output_term(down_pack[0], down_pack[1])
    out_term = output_term(out_pack[0], out_pack[1])
    return lax.psum_scatter(
        (attn_w, attn_g, mlp_w, mlp_g, down_term, out_term),
        ("dp", "heads"),
        scatter_dimension=0,
        tiled=True,
    )


def tensor_total(partial_sum):
    return lax.psum(partial_sum, "tensor")


def block_masks(row_index, row_segment, key_index, key_segment):
    return (row_segment[:, None] == key_segment[None, :]) & (
        key_index[None, :] <= row_index[:, None]
    )


def attend_forward(query_rows, key_rows, value_rows, query_index, query_segment, key_segment):
    total_rows = query_rows.shape[0]
    block_size = min(512, total_rows)
    blocks = total_rows // block_size
    key_index = jnp.arange(key_rows.shape[0], dtype=jnp.int32)
    scale = HEAD_DIM ** (-0.5)

    def one_block(pieces):
        block_query, row_index, row_segment = pieces
        scores = scale * contract_last(block_query, key_rows)
        scores = jnp.where(
            block_masks(row_index, row_segment, key_index, key_segment), scores, -1e30
        )
        highest = jnp.max(scores, axis=1, keepdims=True)
        exponent = jnp.exp(scores - highest)
        totals = jnp.sum(exponent, axis=1, keepdims=True)
        probability = (exponent / totals).astype(jnp.bfloat16)
        output = jnp.dot(probability, value_rows, preferred_element_type=jnp.float32).astype(
            jnp.bfloat16
        )
        return (output, highest[:, 0] + jnp.log(totals[:, 0]))

    outputs, logsum = lax.map(
        one_block,
        (
            query_rows.reshape(blocks, block_size, -1),
            query_index.reshape(blocks, block_size),
            query_segment.reshape(blocks, block_size),
        ),
    )
    return (outputs.reshape(total_rows, -1), logsum.reshape(total_rows))


def attend_backward(
    query_rows, key_rows, value_rows, grad_rows, logsum, query_index, query_segment, key_segment
):
    total_rows = query_rows.shape[0]
    block_size = min(512, total_rows)
    blocks = total_rows // block_size
    key_index = jnp.arange(key_rows.shape[0], dtype=jnp.int32)
    scale = HEAD_DIM ** (-0.5)

    def one_block(running, pieces):
        key_grad, value_grad = running
        block_query, block_grad, row_logsum, row_index, row_segment = pieces
        scores = scale * contract_last(block_query, key_rows)
        scores = jnp.where(
            block_masks(row_index, row_segment, key_index, key_segment), scores, -1e30
        )
        probability = jnp.exp(scores - row_logsum[:, None])
        grad_prob = contract_last(block_grad, value_rows)
        row_dot = jnp.sum(probability * grad_prob, axis=1, keepdims=True)
        grad_scores = (probability * (grad_prob - row_dot)).astype(jnp.bfloat16)
        query_grad = scale * jnp.dot(grad_scores, key_rows, preferred_element_type=jnp.float32)
        key_grad = key_grad + scale * contract_leading_axis(grad_scores, block_query)
        value_grad = value_grad + contract_leading_axis(
            probability.astype(jnp.bfloat16), block_grad
        )
        return ((key_grad, value_grad), query_grad)

    initial = (jnp.zeros(key_rows.shape, jnp.float32), jnp.zeros(value_rows.shape, jnp.float32))
    sums, query_grads = lax.scan(
        one_block,
        initial,
        (
            query_rows.reshape(blocks, block_size, -1),
            grad_rows.reshape(blocks, block_size, -1),
            logsum.reshape(blocks, block_size),
            query_index.reshape(blocks, block_size),
            query_segment.reshape(blocks, block_size),
        ),
    )
    return (query_grads.reshape(total_rows, -1), sums[0], sums[1])


def adamw(weight, first_moment, second_moment, gradient, step_rate):
    first_new = 0.9 * first_moment + 0.1 * gradient
    second_new = 0.95 * second_moment + 0.05 * gradient * gradient
    corrected = first_new / (1.0 - 0.9**STEP) / (jnp.sqrt(second_new / (1.0 - 0.95**STEP)) + 1e-08)
    return (first_new, second_new, weight - step_rate * (corrected + 0.1 * weight))


def body(
    tokens,
    segments,
    cotangent,
    query_weight,
    key_weight,
    value_weight,
    output_weight,
    gate_weight,
    up_weight,
    down_weight,
    norm_gain_pair,
    query_first,
    key_first,
    value_first,
    output_first,
    gate_first,
    up_first,
    down_first,
    gains_first,
    query_second,
    key_second,
    value_second,
    output_second,
    gate_second,
    up_second,
    down_second,
    gains_second,
):
    heads_count = lax.axis_size("heads")
    local_tokens = tokens.shape[1]
    heads_here = query_weight.shape[1] // HEAD_DIM
    kv_here = key_weight.shape[1] // HEAD_DIM
    group_size = HEADS // KV_HEADS
    splits = max(1, heads_count // heads_here)
    split_rows = local_tokens // splits
    seq_length = local_tokens * heads_count
    heads_rank = lax.axis_index("heads")
    split_rank = heads_rank % splits
    full_segments = lax.all_gather(segments, "heads", axis=1, tiled=True)[0]
    token_index = jnp.arange(seq_length, dtype=jnp.int32)
    previous = jnp.concatenate([jnp.full((1,), -1, jnp.int32), full_segments[:-1]])
    starts = lax.cummax(
        jnp.where(full_segments != previous, token_index, jnp.zeros_like(token_index)), axis=0
    )
    positions = token_index - starts
    own_positions = lax.dynamic_slice_in_dim(positions, heads_rank * local_tokens, local_tokens, 0)
    cos_tab, sin_tab = rotary_tables(own_positions)
    query_index = lax.dynamic_index_in_dim(
        token_index.reshape(heads_count, splits, split_rows), split_rank, 1, keepdims=False
    ).reshape(-1)
    query_segment = lax.dynamic_index_in_dim(
        full_segments.reshape(heads_count, splits, split_rows), split_rank, 1, keepdims=False
    ).reshape(-1)

    def to_items(per_head):
        return (
            per_head.reshape(splits, split_rows, per_head.shape[1], HEAD_DIM)
            .transpose(2, 0, 1, 3)
            .reshape(-1, split_rows, HEAD_DIM)
        )

    def kv_items(per_head):
        return jnp.repeat(per_head.transpose(1, 0, 2), group_size * splits, axis=0)

    def from_items(items):
        return (
            items.reshape(heads_here, splits, split_rows, HEAD_DIM)
            .transpose(1, 2, 0, 3)
            .reshape(local_tokens, heads_here * HEAD_DIM)
        )

    def kv_sum(items):
        return (
            items.reshape(kv_here, group_size * splits, local_tokens, HEAD_DIM)
            .sum(axis=1)
            .transpose(1, 0, 2)
        )

    input_rows = tokens[0].astype(jnp.float32)
    attention_inverse_norm = lax.rsqrt(
        jnp.mean(input_rows * input_rows, axis=1, keepdims=True) + EPS
    )
    attention_unit_rows = input_rows * attention_inverse_norm
    attention_joined = jnp.concatenate([query_weight, key_weight, value_weight], axis=1).astype(
        jnp.bfloat16
    )
    attention_norm_gain = norm_gain_pair[0].astype(jnp.bfloat16)
    out_low = output_weight.astype(jnp.bfloat16)
    projected_rows, attention_normalized, attention_gain_value = folded_normalized(
        attention_unit_rows, attention_norm_gain, attention_joined
    )
    query_cols = heads_here * HEAD_DIM
    kv_cols = kv_here * HEAD_DIM
    query_rot = rotate(
        projected_rows[:, :query_cols].reshape(local_tokens, heads_here, HEAD_DIM), cos_tab, sin_tab
    ).astype(jnp.bfloat16)
    key_rot = rotate(
        projected_rows[:, query_cols : query_cols + kv_cols].reshape(
            local_tokens, kv_here, HEAD_DIM
        ),
        cos_tab,
        sin_tab,
    ).astype(jnp.bfloat16)
    value_low = (
        projected_rows[:, query_cols + kv_cols :]
        .reshape(local_tokens, kv_here, HEAD_DIM)
        .astype(jnp.bfloat16)
    )
    query_recv, key_recv, value_recv = (
        lax.all_to_all(to_items(query_rot), "heads", split_axis=0, concat_axis=1, tiled=True),
        lax.all_to_all(kv_items(key_rot), "heads", split_axis=0, concat_axis=1, tiled=True),
        lax.all_to_all(kv_items(value_low), "heads", split_axis=0, concat_axis=1, tiled=True),
    )

    def head_forward(pieces):
        return attend_forward(
            pieces[0], pieces[1], pieces[2], query_index, query_segment, full_segments
        )

    attended, logsum = lax.map(head_forward, (query_recv, key_recv, value_recv))
    attn_out = from_items(
        lax.all_to_all(attended, "heads", split_axis=1, concat_axis=0, tiled=True)
    )
    attn_partial = project_out(attn_out, out_low)
    residual_stream = input_rows + tensor_total(attn_partial)
    feedforward_inverse_norm = lax.rsqrt(
        jnp.mean(residual_stream * residual_stream, axis=1, keepdims=True) + EPS
    )
    feedforward_unit_rows = residual_stream * feedforward_inverse_norm
    feedforward_joined = jnp.concatenate([gate_weight, up_weight], axis=1).astype(jnp.bfloat16)
    gate_up, feedforward_normalized, feedforward_gain = folded_normalized(
        feedforward_unit_rows, norm_gain_pair[1].astype(jnp.bfloat16), feedforward_joined
    )
    ff_here = gate_weight.shape[1]
    gate_proj = gate_up[:, :ff_here]
    up_proj = gate_up[:, ff_here:]
    sigmoid_gate = jax.nn.sigmoid(gate_proj)
    silu_gate = gate_proj * sigmoid_gate
    active = (silu_gate * up_proj).astype(jnp.bfloat16)
    down_low = down_weight.astype(jnp.bfloat16)
    block_out = residual_stream + tensor_total(project_out(active, down_low))
    grad_out = cotangent[0].astype(jnp.float32)
    gradient_reduced = cotangent[0]
    grad_active = project_back(gradient_reduced, down_low)
    grad_gate = grad_active * up_proj * sigmoid_gate * (1.0 + gate_proj * (1.0 - sigmoid_gate))
    grad_up = grad_active * silu_gate
    feedforward_joined_gradient = jnp.concatenate([grad_gate, grad_up], axis=1).astype(jnp.bfloat16)
    feedforward_normalized_gradient = tensor_total(
        normed_back(feedforward_joined_gradient, feedforward_joined)
    )
    feedforward_unit_gradient = feedforward_normalized_gradient * feedforward_gain[None, :]
    grad_resid = grad_out + feedforward_inverse_norm * (
        feedforward_unit_gradient
        - feedforward_unit_rows
        * jnp.mean(feedforward_unit_gradient * feedforward_unit_rows, axis=1, keepdims=True)
    )
    grad_resid_low = grad_resid.astype(jnp.bfloat16)
    grad_attn_out = project_back(grad_resid_low, out_low)
    grad_attn_low = grad_attn_out.astype(jnp.bfloat16).reshape(local_tokens, heads_here, HEAD_DIM)
    grad_recv = lax.all_to_all(
        to_items(grad_attn_low), "heads", split_axis=0, concat_axis=1, tiled=True
    )

    def head_backward(pieces):
        return attend_backward(
            pieces[0],
            pieces[1],
            pieces[2],
            pieces[3],
            pieces[4],
            query_index,
            query_segment,
            full_segments,
        )

    query_grads, key_grads, value_grads = lax.map(
        head_backward, (query_recv, key_recv, value_recv, grad_recv, logsum)
    )
    query_back, key_back, value_back = (
        lax.all_to_all(
            query_grads.astype(jnp.bfloat16), "heads", split_axis=1, concat_axis=0, tiled=True
        ).astype(query_grads.dtype),
        lax.all_to_all(
            key_grads.astype(jnp.bfloat16), "heads", split_axis=1, concat_axis=0, tiled=True
        ).astype(key_grads.dtype),
        lax.all_to_all(
            value_grads.astype(jnp.bfloat16), "heads", split_axis=1, concat_axis=0, tiled=True
        ).astype(value_grads.dtype),
    )
    query_tok = unrotate(
        from_items(query_back).reshape(local_tokens, heads_here, HEAD_DIM), cos_tab, sin_tab
    )
    key_tok = unrotate(kv_sum(key_back), cos_tab, sin_tab)
    value_tok = kv_sum(value_back)
    attention_joined_gradient = jnp.concatenate(
        [
            query_tok.reshape(local_tokens, -1),
            key_tok.reshape(local_tokens, -1),
            value_tok.reshape(local_tokens, -1),
        ],
        axis=1,
    ).astype(jnp.bfloat16)
    grad_normed_part = normed_back(attention_joined_gradient, attention_joined)
    attention_normalized_gradient = tensor_total(grad_normed_part)
    summed = every_grad(
        (
            attention_normalized,
            attention_joined_gradient,
            attention_normalized_gradient,
            attention_unit_rows,
        ),
        (
            feedforward_normalized,
            feedforward_joined_gradient,
            feedforward_normalized_gradient,
            feedforward_unit_rows,
        ),
        (gradient_reduced, active),
        (grad_resid_low, attn_out),
    )
    attn_grads, gain_grad_attn, mlp_grads, gain_grad_mlp = (
        summed[0],
        summed[1],
        summed[2],
        summed[3],
    )
    down_grad = summed[4].T
    output_grad = summed[5].T
    attention_unit_gradient = attention_normalized_gradient * attention_gain_value[None, :]
    input_grad = grad_resid + attention_inverse_norm * (
        attention_unit_gradient
        - attention_unit_rows
        * jnp.mean(attention_unit_gradient * attention_unit_rows, axis=1, keepdims=True)
    )
    query_grad = attn_grads[:, :query_cols]
    key_grad = attn_grads[:, query_cols : query_cols + kv_cols]
    value_grad = attn_grads[:, query_cols + kv_cols :]
    gate_grad = mlp_grads[:, :ff_here]
    up_grad = mlp_grads[:, ff_here:]
    gains_grad = jnp.stack([gain_grad_attn, gain_grad_mlp], axis=0)
    wide_rate = 2.0 * D ** (-0.5)
    query_first_new, query_second_new, query_new = adamw(
        query_weight, query_first, query_second, query_grad, wide_rate
    )
    key_first_new, key_second_new, key_new = adamw(
        key_weight, key_first, key_second, key_grad, wide_rate
    )
    value_first_new, value_second_new, value_new = adamw(
        value_weight, value_first, value_second, value_grad, wide_rate
    )
    output_first_new, output_second_new, output_new = adamw(
        output_weight, output_first, output_second, output_grad, 2.0 * (4 * HEAD_DIM) ** (-0.5)
    )
    gate_first_new, gate_second_new, gate_new = adamw(
        gate_weight, gate_first, gate_second, gate_grad, wide_rate
    )
    up_first_new, up_second_new, up_new = adamw(up_weight, up_first, up_second, up_grad, wide_rate)
    down_first_new, down_second_new, down_new = adamw(
        down_weight, down_first, down_second, down_grad, 2.0 * FF ** (-0.5)
    )
    gains_first_new, gains_second_new, gains_new = adamw(
        norm_gain_pair, gains_first, gains_second, gains_grad, 1.5
    )
    return (
        block_out.astype(jnp.bfloat16)[None],
        input_grad[None],
        query_grad,
        query_first_new,
        query_second_new,
        query_new,
        key_grad,
        key_first_new,
        key_second_new,
        key_new,
        value_grad,
        value_first_new,
        value_second_new,
        value_new,
        output_grad,
        output_first_new,
        output_second_new,
        output_new,
        gate_grad,
        gate_first_new,
        gate_second_new,
        gate_new,
        up_grad,
        up_first_new,
        up_second_new,
        up_new,
        down_grad,
        down_first_new,
        down_second_new,
        down_new,
        gains_grad,
        gains_first_new,
        gains_second_new,
        gains_new,
    )


def solution(mesh):
    in_specs = (
        P("dp", "heads", None),
        P("dp", "heads"),
        P("dp", "heads", None),
        P(("dp", "heads"), "tensor"),
        P(("dp", "heads"), "tensor"),
        P(("dp", "heads"), "tensor"),
        P("tensor", ("dp", "heads")),
        P(("dp", "heads"), "tensor"),
        P(("dp", "heads"), "tensor"),
        P("tensor", ("dp", "heads")),
        P(None, ("dp", "heads")),
        P(("dp", "heads"), "tensor"),
        P(("dp", "heads"), "tensor"),
        P(("dp", "heads"), "tensor"),
        P("tensor", ("dp", "heads")),
        P(("dp", "heads"), "tensor"),
        P(("dp", "heads"), "tensor"),
        P("tensor", ("dp", "heads")),
        P(None, ("dp", "heads")),
        P(("dp", "heads"), "tensor"),
        P(("dp", "heads"), "tensor"),
        P(("dp", "heads"), "tensor"),
        P("tensor", ("dp", "heads")),
        P(("dp", "heads"), "tensor"),
        P(("dp", "heads"), "tensor"),
        P("tensor", ("dp", "heads")),
        P(None, ("dp", "heads")),
    )
    out_specs = (
        P("dp", "heads", None),
        P("dp", "heads", None),
        P(("dp", "heads"), "tensor"),
        P(("dp", "heads"), "tensor"),
        P(("dp", "heads"), "tensor"),
        P(("dp", "heads"), "tensor"),
        P(("dp", "heads"), "tensor"),
        P(("dp", "heads"), "tensor"),
        P(("dp", "heads"), "tensor"),
        P(("dp", "heads"), "tensor"),
        P(("dp", "heads"), "tensor"),
        P(("dp", "heads"), "tensor"),
        P(("dp", "heads"), "tensor"),
        P(("dp", "heads"), "tensor"),
        P("tensor", ("dp", "heads")),
        P("tensor", ("dp", "heads")),
        P("tensor", ("dp", "heads")),
        P("tensor", ("dp", "heads")),
        P(("dp", "heads"), "tensor"),
        P(("dp", "heads"), "tensor"),
        P(("dp", "heads"), "tensor"),
        P(("dp", "heads"), "tensor"),
        P(("dp", "heads"), "tensor"),
        P(("dp", "heads"), "tensor"),
        P(("dp", "heads"), "tensor"),
        P(("dp", "heads"), "tensor"),
        P("tensor", ("dp", "heads")),
        P("tensor", ("dp", "heads")),
        P("tensor", ("dp", "heads")),
        P("tensor", ("dp", "heads")),
        P(None, ("dp", "heads")),
        P(None, ("dp", "heads")),
        P(None, ("dp", "heads")),
        P(None, ("dp", "heads")),
    )
    return jax.shard_map(body, mesh=mesh, in_specs=in_specs, out_specs=out_specs, check_vma=False)
```

profile of v0, /device:TPU:1, one launch (start us, length us, event | category | flops | bytes accessed | tf_op | source)
XLA Modules:
  0.0 5137.2 jit_solution(7105622260240975563)
XLA Ops:
  13.5 158.5 %all-reduce.6 = (bf16[2048]{0:T(1024)(128)(2,1)S(1)}, bf16[2048]{0:T(1024)(128)(2,1)S(1)}) all-reduce(bf16[2048]{0:T(1024)(128)(2,1)S(1)} %dynamic-update-slice, bf16[2048]{0:T(1024)(128)(2,1)S(1)} %dynamic-update-slice.1), channel_id=2, replica_groups=mesh['dp'=2,'heads'=32,'tensor'=2] {'dp','heads'}, use_global_device_ids=true, to_apply=%add | all-reduce | flops 4096 | bytes 16384
  172.1 64.7 %all_gather.25 = s32[1,4096]{1,0:T(1,128)S(1)} all-gather(s32[1,128]{1,0:T(1,128)} %param.32), channel_id=1, replica_groups=mesh['dp'=2,'heads'=32,'tensor'=2] {'heads'}, dimensions={1}, use_global_device_ids=true | all-gather | bytes 16896 | tf_op jit(solution)/shard_map/all_gather | solution.py:262
  239.0 73.7 %all-gather.7.cloned.1.call-done = bf16[2048,1536]{1,0:T(8,128)(2,1)} async-done(((bf16[32,1536]{1,0:T(8,128)(2,1)}), bf16[2048,1536]{1,0:T(8,128)(2,1)}) %all-gather.7.cloned.1.call-update) | async-done | bytes 6291472 | tf_op jit(solution)/shard_map/all_gather | solution.py:80
  362.2 23.9 while.48
  391.8 12.3 reduce.61
  421.8 270.9 %all-gather.9.cloned.1.call-done = bf16[1024,2048]{0,1:T(8,128)(2,1)} async-done(((bf16[1024,32]{0,1:T(8,128)(2,1)}), bf16[1024,2048]{0,1:T(8,128)(2,1)}) %all-gather.9.cloned.1.call-update) | async-done | bytes 4194320 | tf_op jit(solution)/shard_map/all_gather | solution.py:90
  702.4 63.3 %all-reduce.11.cloned.1.call-done = f32[128,2048]{1,0:T(8,128)} async-done(((f32[128,2048]{1,0:T(8,128)}), f32[128,2048]{1,0:T(8,128)}) %all-reduce.11.cloned.1.call-update) | async-done | bytes 1048592 | tf_op jit(solution)/shard_map/psum | solution.py:132
  767.1 722.8 %all-gather.11.cloned.1.call-done = bf16[2048,8192]{1,0:T(8,128)(2,1)} async-done(((bf16[32,8192]{1,0:T(8,128)(2,1)}), bf16[2048,8192]{1,0:T(8,128)(2,1)}) %all-gather.11.cloned.1.call-update) | async-done | bytes 33554448 | tf_op jit(solution)/shard_map/all_gather | solution.py:80
  1490.0 17.2 fusion.73
  1507.2 356.3 %all-gather.13.cloned.1.call-done = bf16[4096,2048]{0,1:T(8,128)(2,1)} async-done(((bf16[4096,32]{0,1:T(8,128)(2,1)}), bf16[4096,2048]{0,1:T(8,128)(2,1)}) %all-gather.13.cloned.1.call-update) | async-done | bytes 16777232 | tf_op jit(solution)/shard_map/all_gather | solution.py:90
  1876.0 17.0 fusion.37
  1893.0 25.7 all-reduce.13.cloned.1.call-done
  1942.9 116.9 %while.49 = (s32[]{:T(128)}, f32[4096,64]{0,1:T(8,128)S(1)}, f32[4096,64]{0,1:T(8,128)S(1)}, bf16[4,512,64]{1,2,0:T(8,128)(2,1)}, s32[4,512]{1,0:T(4,128)S(1)}, ...) while((s32[]{:T(128)}, f32[4096,64]{0,1:T(8,128)S(1)}, ...), condition=%wide.region_14.15_spmd.clone, body=%wide.region_12.14_spmd.clone.sunk | while | flops 1368686080 | bytes 122853680 | solution.py:202
  2065.0 12.5 reduce.64
  2090.0 23.4 reduce.62
  2124.7 12.4 fusion.87
  2141.9 22.4 reduce.63
  2212.7 14.0 convolution_bitcast_fusion
  2226.8 31.2 copy.212
  2259.2 24.9 fusion.36
  2287.1 295.1 %all-reduce.4 = (f32[2048]{0:T(1024)}, f32[2048]{0:T(1024)}) all-reduce(f32[2048]{0:T(1024)S(1)} %copy-done.40, f32[2048]{0:T(1024)} %get-tuple-element.499), channel_id=9, replica_groups=mesh['dp'=2,'heads'=32,'tensor'=2] {'dp','heads'}, use_global_device_ids=true, to_apply=%region_26.27.clone | all-reduce | flops 4096 | bytes 32768
  2592.4 335.8 %reduce-scatter.7.cloned.1.call-done = f32[32,1536]{1,0:T(8,128)} async-done(((f32[2048,1536]{1,0:T(8,128)}), f32[32,1536]{1,0:T(8,128)}) %reduce-scatter.7.cloned.1.call-update) | async-done | bytes 196624 | tf_op jit(solution)/shard_map/reduce_scatter | solution.py:123
  2931.7 762.1 %reduce-scatter.13.cloned.1.call-done = f32[32,4096]{1,0:T(8,128)} async-done(((f32[2048,4096]{1,0:T(8,128)}), f32[32,4096]{1,0:T(8,128)}) %reduce-scatter.13.cloned.1.call-update) | async-done | bytes 524304 | tf_op jit(solution)/shard_map/reduce_scatter | solution.py:123
  3696.6 1430.1 %reduce-scatter.11.cloned.1.call-done = f32[32,8192]{1,0:T(8,128)} async-done(((f32[2048,8192]{1,0:T(8,128)}), f32[32,8192]{1,0:T(8,128)}) %reduce-scatter.11.cloned.1.call-update) | async-done | bytes 1048592 | tf_op jit(solution)/shard_map/reduce_scatter | solution.py:123
  (330 shorter events, 373.7 us)
Async XLA Ops:
  7.2 305.5 %all-gather.7.cloned.1.call-start = ((), (), s32[]{:S(2)}) async-start(), calls=%async_computation.12 | async-start | bytes 6389760 | tf_op jit(solution)/shard_map/all_gather | solution.py:80
  319.1 11.9 all-to-all-start
  331.9 13.8 all-to-all-start.1
  346.6 14.1 all-to-all-start.2
  351.2 341.5 %all-gather.9.cloned.1.call-start = ((), (), s32[]{:S(2)}) async-start(), calls=%async_computation.13 | async-start | bytes 4259840 | tf_op jit(solution)/shard_map/all_gather | solution.py:90
  352.0 413.7 %all-reduce.11.cloned.1.call-start = ((), (), s32[]{:S(2)}) async-start(), calls=%async_computation.14 | async-start | bytes 2097152 | tf_op jit(solution)/shard_map/psum | solution.py:132
  697.4 792.6 %all-gather.11.cloned.1.call-start = ((), (), s32[]{:S(2)}) async-start(), calls=%async_computation.15 | async-start | bytes 34078720 | tf_op jit(solution)/shard_map/all_gather | solution.py:80
  700.4 1163.0 %all-gather.13.cloned.1.call-start = ((), (), s32[]{:S(2)}) async-start(), calls=%async_computation.16 | async-start | bytes 17039360 | tf_op jit(solution)/shard_map/all_gather | solution.py:90
  702.3 1216.5 %all-reduce.13.cloned.1.call-start = ((), (), s32[]{:S(2)}) async-start(), calls=%async_computation.17 | async-start | bytes 2097152 | tf_op jit(solution)/shard_map/psum | solution.py:132
  1925.2 16.6 all-to-all-start.4
  2079.8 36.7 all-to-all-start.5
  2116.5 52.0 %all-to-all-start.7 = ((bf16[32,2,4096]{2,1,0:T(2,128)(2,1)}), bf16[32,2,4096]{2,1,0:T(2,128)(2,1)}, u32[]{:S(2)}, u32[]{:S(2)}) async-start(bf16[32,2,4096]{2,1,0:T(2,128)(2,1)} %reshape.437), calls=%async_computation.7 | async-start | bytes 1048576 | tf_op jit(solution)/shard_map/all_to_all | solution.py:409
  2168.5 17.5 all-to-all-start.6
  2176.6 108.3 %all-reduce.15.cloned.1.call-start = ((), (), s32[]{:S(2)}) async-start(), calls=%async_computation.22 | async-start | bytes 4194304 | tf_op jit(solution)/shard_map/psum | solution.py:132
  2198.6 391.9 %reduce-scatter.9.cloned.1.call-start = ((), (), s32[]{:S(2)}) async-start(), calls=%async_computation.19 | async-start | bytes 8519680 | tf_op jit(solution)/shard_map/reduce_scatter | solution.py:123
  2203.2 725.0 %reduce-scatter.7.cloned.1.call-start = ((), (), s32[]{:S(2)}) async-start(), calls=%async_computation.18 | async-start | bytes 12779520 | tf_op jit(solution)/shard_map/reduce_scatter | solution.py:123
  2211.3 1482.5 %reduce-scatter.13.cloned.1.call-start = ((), (), s32[]{:S(2)}) async-start(), calls=%async_computation.21 | async-start | bytes 34078720 | tf_op jit(solution)/shard_map/reduce_scatter | solution.py:123
  2258.0 2868.7 %reduce-scatter.11.cloned.1.call-start = ((), (), s32[]{:S(2)}) async-start(), calls=%async_computation.20 | async-start | bytes 68157440 | tf_op jit(solution)/shard_map/reduce_scatter | solution.py:123
  2284.1 1409.7 %copy-start.18 = (f32[4096,32]{0,1:T(8,128)S(1)}, f32[4096,32]{0,1:T(8,128)}, u32[]{:S(2)}) copy-start(f32[4096,32]{0,1:T(8,128)} %param.40) | copy-start | bytes 1572868
  2587.9 2538.8 %copy-start.19 = (f32[32,4096]{1,0:T(8,128)S(1)}, f32[32,4096]{1,0:T(8,128)}, u32[]{:S(2)}) copy-start(f32[32,4096]{1,0:T(8,128)} %param.39) | copy-start | bytes 1572868
  2587.9 2538.8 %copy-start.20 = (f32[32,4096]{1,0:T(8,128)S(1)}, f32[32,4096]{1,0:T(8,128)}, u32[]{:S(2)}) copy-start(f32[32,4096]{1,0:T(8,128)} %param.38) | copy-start | bytes 1572868
  2590.5 2536.2 %copy-start.23 = (f32[32,4096]{1,0:T(8,128)S(1)}, f32[32,4096]{1,0:T(8,128)}, u32[]{:S(2)}) copy-start(f32[32,4096]{1,0:T(8,128)} %param.55) | copy-start | bytes 1572868
  2590.5 2536.2 %copy-start.24 = (f32[32,4096]{1,0:T(8,128)S(1)}, f32[32,4096]{1,0:T(8,128)}, u32[]{:S(2)}) copy-start(f32[32,4096]{1,0:T(8,128)} %param.47) | copy-start | bytes 1572868
  2590.5 2536.2 %copy-start.25 = (f32[32,4096]{1,0:T(8,128)S(1)}, f32[32,4096]{1,0:T(8,128)}, u32[]{:S(2)}) copy-start(f32[32,4096]{1,0:T(8,128)} %param.54) | copy-start | bytes 1572868
  (49 other events, 6461.8 us)
Sparse Core Ops, SparseCore 0:
  10.5 302.1 all-gather.6
  354.3 338.3 all-gather.8
  697.5 68.0 all-reduce.10
  767.8 722.1 all-gather.10
  1492.1 371.2 all-gather.12
  1893.2 25.5 all-reduce.12
  2198.8 28.0 all-reduce.14
  2229.9 320.5 reduce-scatter.8
  2553.1 375.1 reduce-scatter.6
  2931.2 762.5 reduce-scatter.12
  3696.4 1430.2 reduce-scatter.10
where the time goes:
time: 5150 us; the launch traced here: 5140 us
  waiting for transfers between devices  4080 us (79%)
  blocking collectives  530 us (10%)
  matrix products  216 us (4%)
  other arithmetic  161 us (3%)
  local copies, waits for them, and re-layouts  96.3 us (2%)
    reduce_scatter x4, waiting for transfers between devices, every_grad(): lax.psum_scatter((attn_w, attn_g, mlp_w, mlp_g, down_term, out_term), ('d...  2530 us
    all_gather x2, waiting for transfers between devices, folded_normalized(): lax.all_gather(weight_portion, ('dp', 'heads'), axis=0, tiled=True)  797 us
    all_gather x2, waiting for transfers between devices, project_out(): lax.all_gather(weight_portion, ('dp', 'heads'), axis=1, tiled=True)  627 us
    unnamed x2, blocking collectives  454 us
  transfers between devices with their start and end apart: 18, of which 14 were waited for; matrix products, arithmetic and copies ran while one was open for 5% of the time, Pallas kernels for 0%

commit v1 on v0

v1 whole, which is shorter than its diff:
```python
import functools
import itertools
import math

import jax
import jax.numpy as jnp
from jax import lax
from jax.experimental import pallas as pl
from jax.experimental.pallas import tpu as pltpu
from jax.sharding import Mesh
from jax.sharding import PartitionSpec as P

D = 2048
FF = 8192
HEADS = 32
KV_HEADS = 8
HEAD_DIM = 64
STEP = 10
EPS = 1e-05

SIZES = {"dp": 2, "x": 4, "z": 4, "yl": 2, "t": 2}
GROUP = ("z", "yl")
CROSS = ("dp", "x")
MEMBERS = 8
HALF = 64
ROWS = 1024
LENGTH = 4096
QB = 256
KB = 512
BF = jnp.bfloat16
F32 = jnp.float32


def shifts(axes):
    return list(itertools.product(*[range(SIZES[a]) for a in axes]))


def place(axes, shift, sign=1):
    index = 0
    for a, s in zip(axes, shift):
        index = index * SIZES[a] + lax.rem(
            lax.axis_index(a) + (s if sign > 0 else SIZES[a] - s), SIZES[a]
        )
    return index


def peer(axes, shift):
    return {
        a: lax.rem(lax.axis_index(a) + s, SIZES[a]) for a, s in zip(axes, shift) if s
    }


def other_core():
    return {"t": 1 - lax.axis_index("t")}


def greet(devices):
    sem = pltpu.get_barrier_semaphore()
    for device in devices:
        pl.semaphore_signal(
            sem, inc=1, device_id=device, device_id_type=pl.DeviceIdType.MESH
        )
    pl.semaphore_wait(sem, len(devices))


def remote(src, dst, send, recv, device):
    return pltpu.make_async_remote_copy(
        src_ref=src,
        dst_ref=dst,
        send_sem=send,
        recv_sem=recv,
        device_id=device,
        device_id_type=pl.DeviceIdType.MESH,
    )


def gather_kernel(with_segments, *refs):
    if with_segments:
        x_ref, seg_ref, out_ref, seg_out, send, recv, tsend, trecv, local, ssend, srecv, xsend, xrecv, slocal = refs
    else:
        x_ref, out_ref, send, recv, tsend, trecv, local = refs
    t = lax.axis_index("t")
    moves = shifts(GROUP)[1:]
    crossings = [(s,) for s in (1, 2, 3)]
    devices = [other_core()] + [peer(GROUP, s) for s in moves]
    if with_segments:
        devices = devices + [peer(("x",), s) for s in crossings]
    greet(devices)
    me = place(GROUP, (0, 0))
    copies = []
    own = pltpu.make_async_copy(x_ref, out_ref.at[me, t], local)
    own.start()
    if with_segments:
        x = lax.axis_index("x")
        seg_own = pltpu.make_async_copy(seg_ref, seg_out.at[x, me], slocal)
        seg_own.start()
        seg_copies = []
        for i, s in enumerate(moves):
            c = remote(seg_ref, seg_out.at[x, me], ssend.at[i], srecv.at[i], peer(GROUP, s))
            c.start()
            seg_copies.append(c)
    for i, s in enumerate(moves):
        c = remote(x_ref, out_ref.at[me, t], send.at[i], recv.at[i], peer(GROUP, s))
        c.start()
        copies.append(c)
    c = remote(x_ref, out_ref.at[me, t], tsend.at[7], trecv.at[7], other_core())
    c.start()
    passed = [c]
    if with_segments:
        seg_own.wait()
        for c in seg_copies:
            c.wait()
        crossed = []
        for i, s in enumerate(crossings):
            c = remote(seg_out.at[x], seg_out.at[x], xsend.at[i], xrecv.at[i], peer(("x",), s))
            c.start()
            crossed.append(c)
    for i, s in enumerate(moves):
        copies[i].wait_recv()
        source = place(GROUP, s, -1)
        c = remote(
            out_ref.at[source, t], out_ref.at[source, t], tsend.at[i], trecv.at[i], other_core()
        )
        c.start()
        passed.append(c)
    own.wait()
    for c in copies:
        c.wait_send()
    for c in passed:
        c.wait()
    if with_segments:
        for c in crossed:
            c.wait()


def gather_tokens(x, segments=None):
    with_segments = segments is not None
    wide = x.shape[1]
    dma = pltpu.SemaphoreType.DMA
    out_shape = [jax.ShapeDtypeStruct((MEMBERS, 2, HALF, wide), x.dtype)]
    scratch = [dma((7,)), dma((7,)), dma((8,)), dma((8,)), dma]
    args = [x]
    if with_segments:
        out_shape.append(jax.ShapeDtypeStruct((4, MEMBERS, 8, 128), jnp.int32))
        scratch = scratch + [dma((7,)), dma((7,)), dma((3,)), dma((3,)), dma]
        args.append(segments)
    hbm = pl.BlockSpec(memory_space=pl.ANY)
    out = pl.pallas_call(
        functools.partial(gather_kernel, with_segments),
        out_shape=out_shape,
        in_specs=[hbm] * len(args),
        out_specs=[hbm] * len(out_shape),
        scratch_shapes=scratch,
        compiler_params=pltpu.CompilerParams(
            collective_id=1 if with_segments else 2, has_side_effects=True
        ),
        cost_estimate=pl.CostEstimate(flops=0, bytes_accessed=60_000_000, transcendentals=0),
        name="gather_tokens_first" if with_segments else "gather_tokens",
    )(*args)
    gathered = out[0].reshape(ROWS, wide)
    return (gathered, out[1]) if with_segments else gathered


def scatter_kernel(p_ref, out_ref, mine, theirs, sums, land, lsem, tsend, trecv, send, recv):
    t = lax.axis_index("t")
    moves = shifts(GROUP)
    order = moves[1:] + moves[:1]
    greet([other_core()] + [peer(GROUP, s) for s in moves[1:]])
    loads, swaps = [], []
    for i, s in enumerate(order):
        chunk = place(GROUP, s)
        c = remote(p_ref.at[chunk, 1 - t], theirs.at[i], tsend.at[i], trecv.at[i], other_core())
        c.start()
        swaps.append(c)
        c = pltpu.make_async_copy(p_ref.at[chunk, t], mine.at[i], lsem.at[i])
        c.start()
        loads.append(c)
    copies = []
    for i, s in enumerate(order[:7]):
        loads[i].wait()
        swaps[i].wait_recv()
        sums[i] = (mine[i].astype(F32) + theirs[i].astype(F32)).astype(BF)
        c = remote(sums.at[i], land.at[i], send.at[i], recv.at[i], peer(GROUP, s))
        c.start()
        copies.append(c)
    loads[7].wait()
    swaps[7].wait_recv()
    out_ref[...] = mine[7].astype(F32) + theirs[7].astype(F32)
    for i in range(7):
        copies[i].wait_recv()
        out_ref[...] += land[i].astype(F32)
    for c in copies:
        c.wait_send()
    for c in swaps:
        c.wait_send()


def scatter_sum(partial_sum):
    wide = partial_sum.shape[1]
    dma = pltpu.SemaphoreType.DMA
    slots = (MEMBERS, HALF, wide)
    return pl.pallas_call(
        scatter_kernel,
        out_shape=jax.ShapeDtypeStruct((HALF, wide), F32),
        in_specs=[pl.BlockSpec(memory_space=pl.ANY)],
        out_specs=pl.BlockSpec(memory_space=pltpu.VMEM),
        scratch_shapes=[
            pltpu.VMEM(slots, BF),
            pltpu.VMEM(slots, BF),
            pltpu.VMEM((7, HALF, wide), BF),
            pltpu.VMEM((7, HALF, wide), BF),
            dma((8,)),
            dma((8,)),
            dma((8,)),
            dma((7,)),
            dma((7,)),
        ],
        compiler_params=pltpu.CompilerParams(
            collective_id=3, has_side_effects=True, vmem_limit_bytes=32 * 2**20
        ),
        cost_estimate=pl.CostEstimate(flops=0, bytes_accessed=60_000_000, transcendentals=0),
        name="scatter_sum",
    )(partial_sum.reshape(MEMBERS, 2, HALF, wide))


def gather_x_kernel(x_ref, out_ref, send, recv, local):
    moves = [(s,) for s in (1, 2, 3)]
    greet([peer(("x",), s) for s in moves])
    me = lax.axis_index("x")
    own = pltpu.make_async_copy(x_ref, out_ref.at[me], local)
    own.start()
    copies = []
    for i, s in enumerate(moves):
        c = remote(x_ref, out_ref.at[me], send.at[i], recv.at[i], peer(("x",), s))
        c.start()
        copies.append(c)
    own.wait()
    for c in copies:
        c.wait()


def gather_x(x):
    dma = pltpu.SemaphoreType.DMA
    hbm = pl.BlockSpec(memory_space=pl.ANY)
    out = pl.pallas_call(
        gather_x_kernel,
        out_shape=jax.ShapeDtypeStruct((4,) + x.shape, x.dtype),
        in_specs=[hbm],
        out_specs=hbm,
        scratch_shapes=[dma((3,)), dma((3,)), dma],
        compiler_params=pltpu.CompilerParams(collective_id=4, has_side_effects=True),
        cost_estimate=pl.CostEstimate(flops=0, bytes_accessed=30_000_000, transcendentals=0),
        name="gather_keys",
    )(x)
    return out.reshape(4 * x.shape[0], x.shape[1])


def scatter_x_kernel(p_ref, out_ref, mine, land, lsem, send, recv):
    moves = [(s,) for s in (1, 2, 3)]
    greet([peer(("x",), s) for s in moves])
    me = lax.axis_index("x")
    own = pltpu.make_async_copy(p_ref.at[me], mine, lsem)
    own.start()
    copies = []
    for i, s in enumerate(moves):
        c = remote(p_ref.at[place(("x",), s)], land.at[i], send.at[i], recv.at[i], peer(("x",), s))
        c.start()
        copies.append(c)
    own.wait()
    out_ref[...] = mine[...].astype(F32)
    for i in range(3):
        copies[i].wait()
        out_ref[...] += land[i].astype(F32)


def scatter_x(p):
    dma = pltpu.SemaphoreType.DMA
    wide = p.shape[1]
    return pl.pallas_call(
        scatter_x_kernel,
        out_shape=jax.ShapeDtypeStruct((ROWS, wide), F32),
        in_specs=[pl.BlockSpec(memory_space=pl.ANY)],
        out_specs=pl.BlockSpec(memory_space=pltpu.VMEM),
        scratch_shapes=[
            pltpu.VMEM((ROWS, wide), BF),
            pltpu.VMEM((3, ROWS, wide), BF),
            dma,
            dma((3,)),
            dma((3,)),
        ],
        compiler_params=pltpu.CompilerParams(collective_id=5, has_side_effects=True),
        cost_estimate=pl.CostEstimate(flops=0, bytes_accessed=30_000_000, transcendentals=0),
        name="scatter_key_grads",
    )(p.reshape(4, ROWS, wide))


def abt(left, right):
    return lax.dot_general(left, right, (((1,), (1,)), ((), ())), preferred_element_type=F32)


def atb(left, right):
    return lax.dot_general(left, right, (((0,), (0,)), ((), ())), preferred_element_type=F32)


def attend_kernel(lo_ref, hi_ref, q_ref, kv_ref, kvt_ref, qi_ref, st_ref, o_ref, lse_ref):
    i = pl.program_id(0)
    q = q_ref[...]
    row, start = qi_ref[...], st_ref[...]
    wide = q.shape[0]

    def step(j, carry):
        top, total, acc = carry
        base = pl.multiple_of(j * KB, KB)
        s = abt(kv_ref[pl.ds(base, KB), :], q)
        key = base + lax.broadcasted_iota(jnp.int32, (KB, wide), 0)
        s = jnp.where((key <= row) & (key >= start), s, -1e30)
        new_top = jnp.maximum(top, jnp.max(s, axis=0, keepdims=True))
        p = jnp.exp(s - new_top)
        fade = jnp.exp(top - new_top)
        total = total * fade + jnp.sum(p, axis=0, keepdims=True)
        acc = acc * fade + jnp.dot(
            kvt_ref[:, pl.ds(base, KB)], p.astype(BF), preferred_element_type=F32
        )
        return (new_top, total, acc)

    init = (
        jnp.full((1, wide), -1e30, F32),
        jnp.zeros((1, wide), F32),
        jnp.zeros((2 * HEAD_DIM, wide), F32),
    )
    top, total, acc = lax.fori_loop(lo_ref[i], hi_ref[i], step, init)
    o_ref[...] = acc / total
    lse_ref[...] = top + jnp.log(total)


def attend_back_kernel(
    lo_ref, hi_ref, q_ref, g_ref, kv_ref, kvt_ref, qi_ref, st_ref, lse_ref, dot_ref, dq_ref, dkv_ref, acc_ref
):
    i = pl.program_id(0)
    q, g = q_ref[...], g_ref[...]
    row, start, lse, row_dot = qi_ref[...], st_ref[...], lse_ref[...], dot_ref[...]
    wide = q.shape[0]

    @pl.when(i == 0)
    def _():
        acc_ref[...] = jnp.zeros_like(acc_ref)

    def step(j, dq):
        base = pl.multiple_of(j * KB, KB)
        kv = kv_ref[pl.ds(base, KB), :]
        s = abt(kv, q)
        key = base + lax.broadcasted_iota(jnp.int32, (KB, wide), 0)
        s = jnp.where((key <= row) & (key >= start), s, -1e30)
        p = jnp.exp(s - lse)
        ds = (p * (abt(kv, g) - row_dot)).astype(BF)
        acc_ref[pl.ds(base, KB), :] += jnp.dot(ds, q, preferred_element_type=F32) + jnp.dot(
            p.astype(BF), g, preferred_element_type=F32
        )
        return dq + jnp.dot(kvt_ref[:, pl.ds(base, KB)], ds, preferred_element_type=F32)

    dq_ref[...] = lax.fori_loop(
        lo_ref[i], hi_ref[i], step, jnp.zeros((2 * HEAD_DIM, wide), F32)
    )

    @pl.when(i == pl.num_programs(0) - 1)
    def _():
        dkv_ref[...] = acc_ref[...].astype(BF)


def whole(shape):
    return pl.BlockSpec(shape, lambda i: (0,) * len(shape))


def block(rows, columns):
    return pl.BlockSpec((None, rows, columns), lambda i: (i, 0, 0))


BLOCKS = ROWS // QB
WIDE = 2 * QB
SCALARS = pl.BlockSpec(memory_space=pltpu.SMEM)


def attend(lo, hi, q, kv, kvt, row, start):
    return pl.pallas_call(
        attend_kernel,
        grid=(BLOCKS,),
        out_shape=[
            jax.ShapeDtypeStruct((BLOCKS, 128, WIDE), F32),
            jax.ShapeDtypeStruct((BLOCKS, 1, WIDE), F32),
        ],
        in_specs=[
            SCALARS,
            SCALARS,
            block(WIDE, 128),
            whole((LENGTH, 128)),
            whole((128, LENGTH)),
            block(1, WIDE),
            block(1, WIDE),
        ],
        out_specs=[block(128, WIDE), block(1, WIDE)],
        compiler_params=pltpu.CompilerParams(vmem_limit_bytes=48 * 2**20),
        cost_estimate=pl.CostEstimate(
            flops=2_000_000_000, bytes_accessed=60_000_000, transcendentals=4_000_000
        ),
        name="attend",
    )(lo, hi, q, kv, kvt, row, start)


def attend_back(lo, hi, q, g, kv, kvt, row, start, lse, row_dot):
    return pl.pallas_call(
        attend_back_kernel,
        grid=(BLOCKS,),
        out_shape=[
            jax.ShapeDtypeStruct((BLOCKS, 128, WIDE), F32),
            jax.ShapeDtypeStruct((LENGTH, 128), BF),
        ],
        in_specs=[
            SCALARS,
            SCALARS,
            block(WIDE, 128),
            block(WIDE, 128),
            whole((LENGTH, 128)),
            whole((128, LENGTH)),
            block(1, WIDE),
            block(1, WIDE),
            block(1, WIDE),
            block(1, WIDE),
        ],
        out_specs=[block(128, WIDE), whole((LENGTH, 128))],
        scratch_shapes=[pltpu.VMEM((LENGTH, 128), F32)],
        compiler_params=pltpu.CompilerParams(vmem_limit_bytes=48 * 2**20),
        cost_estimate=pl.CostEstimate(
            flops=5_000_000_000, bytes_accessed=120_000_000, transcendentals=4_000_000
        ),
        name="attend_back",
    )(lo, hi, q, g, kv, kvt, row, start, lse, row_dot)


def permute(x, axes, shift):
    count = math.prod(SIZES[a] for a in axes)
    pairs = []
    for source, at in enumerate(shifts(axes)):
        target = 0
        for a, c, s in zip(axes, at, shift):
            target = target * SIZES[a] + (c + s) % SIZES[a]
        pairs.append((source, target))
    assert len(pairs) == count
    return lax.ppermute(x, axes, pairs)


def swap_cores(x):
    return lax.ppermute(x, "t", [(0, 1), (1, 0)])


def gather_over(x, axes):
    moves = shifts(axes)
    out = jnp.zeros((len(moves),) + x.shape, x.dtype)
    out = lax.dynamic_update_index_in_dim(out, x, place(axes, moves[0]), 0)
    for s in moves[1:]:
        out = lax.dynamic_update_index_in_dim(out, permute(x, axes, s), place(axes, s, -1), 0)
    return out


def sum_over(x, axes):
    moves = shifts(axes)
    total = lax.dynamic_index_in_dim(x, place(axes, moves[0]), 0, keepdims=False).astype(F32)
    for s in moves[1:]:
        chunk = lax.dynamic_index_in_dim(x, place(axes, s), 0, keepdims=False)
        total = total + permute(chunk, axes, s).astype(F32)
    return total


def deal(x):
    return lax.all_to_all(x, GROUP, split_axis=0, concat_axis=0, tiled=True)


def spread(weight_slots):
    dealt = deal(weight_slots)
    wide = weight_slots.shape[2]
    return gather_over(dealt.reshape(MEMBERS * 32, wide), CROSS).reshape(D, wide)


def collect(gradient):
    wide = gradient.shape[1]
    own = sum_over(gradient.reshape(8, 256, wide), CROSS)
    return deal(own.astype(BF).reshape(MEMBERS, 32, wide)).astype(F32)


def rope_frequency():
    half_size = HEAD_DIM // 2
    base_freq = 500000.0 ** (-(jnp.arange(half_size, dtype=F32) * 2.0 / HEAD_DIM))
    wavelength = 2.0 * math.pi / base_freq
    smooth = (8192.0 / wavelength - 1.0) / 3.0
    blended = (1.0 - smooth) * base_freq / 32.0 + smooth * base_freq
    return jnp.where(
        wavelength < 2048.0, base_freq, jnp.where(wavelength > 8192.0, base_freq / 32.0, blended)
    )


def rotate(values, cos_tab, sin_tab):
    rows = values.shape[0]
    v = values.reshape(rows, -1, 2, HEAD_DIM // 2)
    a, b = v[:, :, 0], v[:, :, 1]
    c, s = cos_tab[:, None, :], sin_tab[:, None, :]
    return jnp.stack([a * c - b * s, b * c + a * s], axis=2).reshape(rows, -1)


def adamw(weight, first_moment, second_moment, gradient, step_rate):
    first_new = 0.9 * first_moment + 0.1 * gradient
    second_new = 0.95 * second_moment + 0.05 * gradient * gradient
    corrected = first_new / (1.0 - 0.9**STEP) / (jnp.sqrt(second_new / (1.0 - 0.95**STEP)) + 1e-08)
    return (first_new, second_new, weight - step_rate * (corrected + 0.1 * weight))


def slots(w, columns):
    return w.reshape(w.shape[0], -1, columns).transpose(1, 0, 2)


def unslots(g):
    return g.transpose(1, 0, 2).reshape(g.shape[1], -1)


def heads_apart(x):
    return x.reshape(BLOCKS, QB, 2, HEAD_DIM).transpose(0, 2, 1, 3).reshape(BLOCKS, WIDE, HEAD_DIM)


def heads_beside(x):
    return x.reshape(BLOCKS, HEAD_DIM, 2, QB).transpose(0, 3, 2, 1).reshape(ROWS, 2 * HEAD_DIM)


def body(
    tokens,
    segments,
    cotangent,
    query_weight,
    key_weight,
    value_weight,
    output_weight,
    gate_weight,
    up_weight,
    down_weight,
    norm_gain_pair,
    query_first,
    key_first,
    value_first,
    output_first,
    gate_first,
    up_first,
    down_first,
    gains_first,
    query_second,
    key_second,
    value_second,
    output_second,
    gate_second,
    up_second,
    down_second,
    gains_second,
):
    t = lax.axis_index("t")
    x_place = lax.axis_index("x")

    gains = norm_gain_pair.astype(BF).astype(F32)
    gain_a, gain_m = gains[0][:, None], gains[1][:, None]
    low = lambda w: w.astype(BF).astype(F32)
    fold = lambda g, w: (g * low(w)).astype(BF)
    twice = lambda w: jnp.repeat(slots(w, HEAD_DIM), 2, axis=0)
    attn_slots = jnp.concatenate(
        [
            slots(fold(gain_a, query_weight), 128),
            twice(fold(gain_a, key_weight)),
            twice(fold(gain_a, value_weight)),
            slots(output_weight.astype(BF).T, 128),
        ],
        axis=2,
    )
    mlp_slots = jnp.concatenate(
        [
            slots(fold(gain_m, gate_weight), 512),
            slots(fold(gain_m, up_weight), 512),
            slots(down_weight.astype(BF).T, 512),
        ],
        axis=2,
    )
    attn_w = spread(attn_slots)
    mlp_w = spread(mlp_slots)
    w_qkv, w_out = attn_w[:, :256], attn_w[:, 256:]
    w_gate_up, w_down = mlp_w[:, :1024], mlp_w[:, 1024:]

    rows = lax.dynamic_slice_in_dim(tokens[0], t * HALF, HALF, 0).astype(F32)
    inv_a = lax.rsqrt(jnp.mean(rows * rows, axis=1, keepdims=True) + EPS)
    unit_a = rows * inv_a
    all_a, seg = gather_tokens(unit_a.astype(BF), jnp.broadcast_to(segments, (8, 128)))
    segment = seg[:, :, 0, :].reshape(LENGTH)
    index = jnp.arange(LENGTH, dtype=jnp.int32)
    previous = jnp.concatenate([jnp.full((1,), -1, jnp.int32), segment[:-1]])
    starts = lax.cummax(jnp.where(segment != previous, index, 0), axis=0)
    first_row = x_place * ROWS
    own_start = lax.dynamic_slice_in_dim(starts, first_row, ROWS, 0)
    own_index = first_row + jnp.arange(ROWS, dtype=jnp.int32)
    angles = (own_index - own_start).astype(F32)[:, None] * rope_frequency()[None, :]
    cos_tab, sin_tab = jnp.cos(angles), jnp.sin(angles)
    lo = own_start.reshape(BLOCKS, QB)[:, 0] // KB
    hi = (first_row + (jnp.arange(BLOCKS, dtype=jnp.int32) + 1) * QB + KB - 1) // KB
    by_block = lambda v: jnp.concatenate([v.reshape(BLOCKS, 1, QB)] * 2, axis=2)
    row_ids, row_starts = by_block(own_index), by_block(own_start)

    qkv = jnp.dot(all_a, w_qkv, preferred_element_type=F32)
    rotated = rotate(qkv[:, :192], cos_tab, sin_tab).astype(BF)
    kv_own = jnp.concatenate([rotated[:, 128:], qkv[:, 192:].astype(BF)], axis=1)
    kv = gather_x(kv_own)
    kvt = kv.T
    scale = HEAD_DIM ** (-0.5)
    q_low = heads_apart(rotated[:, :128])
    nothing = jnp.zeros_like(q_low)
    q_wide = jnp.concatenate([q_low * jnp.asarray(scale, BF), nothing], axis=2)
    o_cols, lse = attend(lo, hi, q_wide, kv, kvt, row_ids, row_starts)
    o_full = heads_beside(o_cols[:, HEAD_DIM:])
    o_low = o_full.astype(BF)

    resid = rows + scatter_sum(abt(o_low, w_out).astype(BF))
    inv_m = lax.rsqrt(jnp.mean(resid * resid, axis=1, keepdims=True) + EPS)
    unit_m = resid * inv_m
    all_m = gather_tokens(unit_m.astype(BF))
    gate_up = jnp.dot(all_m, w_gate_up, preferred_element_type=F32)
    gate, up = gate_up[:, :512], gate_up[:, 512:]
    sig = jax.nn.sigmoid(gate)
    silu = gate * sig
    act = (silu * up).astype(BF)

    cot_half = lax.dynamic_slice_in_dim(cotangent[0], t * HALF, HALF, 0)
    cot_own = gather_over(cot_half, GROUP)
    cot_other = swap_cores(cot_own)
    all_g = jnp.where(
        t == 0, jnp.stack([cot_own, cot_other], axis=1), jnp.stack([cot_other, cot_own], axis=1)
    ).reshape(ROWS, D)

    g_act = jnp.dot(all_g, w_down, preferred_element_type=F32)
    g_gate = g_act * up * sig * (1.0 + gate * (1.0 - sig))
    g_up = g_act * silu
    g_gate_up = jnp.concatenate([g_gate, g_up], axis=1).astype(BF)
    g_unit_m = scatter_sum(abt(g_gate_up, w_gate_up).astype(BF))
    grad_out = cot_half.astype(F32)
    g_resid = grad_out + inv_m * (
        g_unit_m - unit_m * jnp.mean(g_unit_m * unit_m, axis=1, keepdims=True)
    )
    all_r = gather_tokens(g_resid.astype(BF))

    mlp_grad = jnp.concatenate([atb(all_m, g_gate_up), atb(all_g, act)], axis=1).astype(BF)
    mlp_sum = collect(mlp_grad)

    down = abt(act, w_down).astype(BF).reshape(MEMBERS, 2, HALF, D)
    pick = lambda v, i: lax.dynamic_index_in_dim(v, i, 1, keepdims=False)
    down_pair = pick(down, t).astype(F32) + swap_cores(pick(down, 1 - t)).astype(F32)
    out_half = (resid + sum_over(down_pair.astype(BF), GROUP)).astype(BF)
    halves = lambda own: jnp.where(
        t == 0,
        jnp.concatenate([own, swap_cores(own)], axis=0),
        jnp.concatenate([swap_cores(own), own], axis=0),
    )
    block_out = halves(out_half)

    g_o = jnp.dot(all_r, w_out, preferred_element_type=F32).astype(BF)
    row_dot = (
        (o_full * g_o.astype(F32))
        .reshape(BLOCKS, QB, 2, HEAD_DIM)
        .sum(axis=3)
        .transpose(0, 2, 1)
        .reshape(BLOCKS, 1, WIDE)
    )
    g_wide = jnp.concatenate([nothing, heads_apart(g_o)], axis=2)
    dq_cols, dkv = attend_back(
        lo, hi, q_wide, g_wide, kv, kvt, row_ids, row_starts, lse, row_dot
    )
    g_kv = scatter_x(dkv)
    g_q = heads_beside(dq_cols[:, :HEAD_DIM]) * scale
    g_turned = rotate(jnp.concatenate([g_q, g_kv[:, :HEAD_DIM]], axis=1), cos_tab, -sin_tab)
    g_qkv = jnp.concatenate([g_turned, g_kv[:, HEAD_DIM:]], axis=1).astype(BF)
    attn_grad = jnp.concatenate([atb(all_a, g_qkv), atb(all_r, o_low)], axis=1).astype(BF)
    attn_sum = collect(attn_grad)
    g_unit_a = scatter_sum(abt(g_qkv, w_qkv).astype(BF))
    input_half = g_resid + inv_a * (
        g_unit_a - unit_a * jnp.mean(g_unit_a * unit_a, axis=1, keepdims=True)
    )
    input_grad = halves(input_half)

    pairs = lambda g: unslots(g.reshape(4, 2, 32, HEAD_DIM).sum(axis=1))
    q_sum = unslots(attn_sum[:, :, :128])
    k_sum = pairs(attn_sum[:, :, 128:192])
    v_sum = pairs(attn_sum[:, :, 192:256])
    gate_sum = unslots(mlp_sum[:, :, :512])
    up_sum = unslots(mlp_sum[:, :, 512:1024])
    dots = lambda g, w: jnp.sum(g * low(w), axis=1)
    gains_half = jnp.stack(
        [
            dots(q_sum, query_weight) + dots(k_sum, key_weight) + dots(v_sum, value_weight),
            dots(gate_sum, gate_weight) + dots(up_sum, up_weight),
        ],
        axis=0,
    )
    gains_grad = gains_half + swap_cores(gains_half)
    query_grad, key_grad, value_grad = gain_a * q_sum, gain_a * k_sum, gain_a * v_sum
    gate_grad, up_grad = gain_m * gate_sum, gain_m * up_sum
    output_grad = unslots(attn_sum[:, :, 256:]).T
    down_grad = unslots(mlp_sum[:, :, 1024:]).T
    wide_rate = 2.0 * D ** (-0.5)
    outs = [block_out[None], input_grad[None]]
    for weight, first, second, grad, rate in (
        (query_weight, query_first, query_second, query_grad, wide_rate),
        (key_weight, key_first, key_second, key_grad, wide_rate),
        (value_weight, value_first, value_second, value_grad, wide_rate),
        (output_weight, output_first, output_second, output_grad, 2.0 * (4 * HEAD_DIM) ** (-0.5)),
        (gate_weight, gate_first, gate_second, gate_grad, wide_rate),
        (up_weight, up_first, up_second, up_grad, wide_rate),
        (down_weight, down_first, down_second, down_grad, 2.0 * FF ** (-0.5)),
        (norm_gain_pair, gains_first, gains_second, gains_grad, 1.5),
    ):
        outs.append(grad)
        outs.extend(adamw(weight, first, second, grad, rate))
    return tuple(outs)


def solution(mesh):
    split = Mesh(
        mesh.devices.reshape(tuple(SIZES.values())), tuple(SIZES)
    )
    heads = ("x", "z", "yl")
    every = ("dp", "x", "z", "yl")
    acts = P("dp", heads, None)
    rows_cut = P(every, "t")
    columns_cut = P("t", every)
    gains = P(None, every)
    weights = (rows_cut,) * 3 + (columns_cut,) + (rows_cut,) * 2 + (columns_cut, gains)
    in_specs = (acts, P("dp", heads), acts) + weights * 3
    out_specs = (acts, acts) + tuple(spec for spec in weights for _ in range(4))
    return jax.shard_map(
        body, mesh=split, in_specs=in_specs, out_specs=out_specs, check_vma=False
    )
```

time: 5150 us -> 709 us (0.14)
  waiting for transfers between devices: 4080 us -> 142 us
  blocking collectives: 530 us -> 0 us
  Pallas kernels: 0 us -> 261 us
  matrix products: 216 us -> 42.3 us
  other arithmetic: 161 us -> 39.7 us
  starting transfers between devices: 41.5 us -> 119 us
    reduce_scatter x4 -> x0, waiting for transfers between devices: 2530 us -> none  [every_grad(): lax.psum_scatter((attn_w, attn_g, mlp_w, mlp_g, down_term, out_term), ('d...]
    all_gather x4 -> x0, waiting for transfers between devices: 1420 us -> none  [the longest x2 797 us: folded_normalized(): lax.all_gather(weight_portion, ('dp', 'heads'), axis=0, tiled=True)]
    unnamed x2 -> x0, blocking collectives: 454 us -> none
    pallas_call x0 -> x10, Pallas kernels: none -> 261 us  [the longest x3 107 us: gather_tokens(): pl.pallas_call(functools.partial(gather_kernel, with_segments), out_shape...]
    dot_general x40 -> x12, matrix products: 216 us -> 42.3 us  [the longest x4 14.6 us: atb(): lax.dot_general(left, right, (((0,), (0,)), ((), ())), preferred_element_...]
    ppermute x0 -> x47, starting transfers between devices: none -> 103 us  [the longest x42 77.9 us: permute(): return lax.ppermute(x, axes, pairs)]
    psum x3 -> x0, waiting for transfers between devices: 89 us -> none  [tensor_total(): return lax.psum(partial_sum, 'tensor')]
    ppermute x0 -> x47, waiting for transfers between devices: none -> 73.9 us  [the longest x42 73.9 us: permute(): return lax.ppermute(x, axes, pairs)]
  transfers between devices with their start and end apart: 18 -> 51, of which waited for: 14 -> 8; matrix products, arithmetic and copies ran while one was open for 5% -> 16% of each run, Pallas kernels for 0% -> 24%
where the time goes in v1:
time: 709 us; the launch traced here: 700 us
  Pallas kernels  261 us (37%)
  waiting for transfers between devices  142 us (20%)
  starting transfers between devices  119 us (17%)
  local copies, waits for them, and re-layouts  94.1 us (13%)
  matrix products  42.3 us (6%)
  other arithmetic  39.7 us (6%)
    pallas_call x3, Pallas kernels, gather_tokens(): pl.pallas_call(functools.partial(gather_kernel, with_segments), out_shape...  107 us
    pallas_call x3, Pallas kernels, scatter_sum(): pl.pallas_call(scatter_kernel, out_shape=jax.ShapeDtypeStruct((HALF, wide...  102 us
    ppermute x42, starting transfers between devices, permute(): return lax.ppermute(x, axes, pairs)  77.9 us
    ppermute x42, waiting for transfers between devices, permute(): return lax.ppermute(x, axes, pairs)  73.9 us
    all_to_all x4, waiting for transfers between devices, deal(): return lax.all_to_all(x, GROUP, split_axis=0, concat_axis=0, tiled=True)  67.8 us
    pallas_call x1, Pallas kernels, scatter_x(): pl.pallas_call(scatter_x_kernel, out_shape=jax.ShapeDtypeStruct((ROWS, wi...  26.7 us
    dot_general x4, local copies, waits for them, and re-layouts, atb(): lax.dot_general(left, right, (((0,), (0,)), ((), ())), preferred_element_...  25.7 us
    ppermute x5, starting transfers between devices, swap_cores(): return lax.ppermute(x, 't', [(0, 1), (1, 0)])  24.9 us
  transfers between devices with their start and end apart: 51, of which 8 were waited for; matrix products, arithmetic and copies ran while one was open for 16% of the time, Pallas kernels for 24%

profile of v1, /device:TPU:1, one launch (start us, length us, event | category | flops | bytes accessed | tf_op | source)
XLA Modules:
  0.0 700.5 jit_solution(4498233141423683299)
XLA Ops:
  19.0 43.4 %gather_tokens_first.1 = (bf16[8,2,64,2048]{3,2,1,0:T(8,128)(2,1)}, s32[4,8,8,128]{3,2,1,0:T(8,128)}) custom-call(bf16[64,2048]{1,0:T(8,128)(2,1)} %fusion.37.refs_0_, s32[8,128]{1,0:T(8,128)} %broadcast_in_dim.113.refs_1_), custom_call_target="tpu_custom_call" | custom-call | bytes 60000000 | tf_op jit(solution)/shard_map/gather_tokens_first/pallas_call | solution.py:148
  67.1 6.3 copy.189
  105.0 4.7 collective-permute-start.5
  122.8 14.1 %gather_keys.1 = bf16[4,1024,128]{2,1,0:T(8,128)(2,1)} custom-call(bf16[1024,128]{1,0:T(8,128)(2,1)} %pad_maximum_fusion.10.x_ref), custom_call_target="tpu_custom_call" | custom-call | bytes 30000000 | tf_op jit(solution)/shard_map/gather_keys/pallas_call | solution.py:245
  149.0 33.0 %scatter_sum.3 = f32[64,2048]{1,0:T(8,128)S(1)} custom-call(bf16[8,2,64,2048]{3,2,1,0:T(8,128)(2,1)S(1)} %bitcast.288), custom_call_target="tpu_custom_call" | custom-call | bytes 60000000 | tf_op jit(solution)/shard_map/scatter_sum/pallas_call | solution.py:202
  182.8 12.2 %collective-permute-start.8 = (bf16[256,1536]{1,0:T(8,128)(2,1)}, bf16[256,1536]{1,0:T(8,128)(2,1)}, u32[]{:S(2)}, u32[]{:S(2)}) collective-permute-start(bf16[256,1536]{1,0:T(8,128)(2,1)} %bitcast.42), channel_id=1, source_target_pairs={{0,32},{16,48},{32,0},{48,16},{64,96},{80,112},{96,64},{112,80},{1... | collective-permute-start | bytes 2359304 | tf_op jit(solution)/shard_map/ppermute | solution.py:448
  199.9 31.2 %gather_tokens.2 = bf16[8,2,64,2048]{3,2,1,0:T(8,128)(2,1)} custom-call(bf16[64,2048]{1,0:T(8,128)(2,1)} %multiply_convert_fusion.3.refs_0_), custom_call_target="tpu_custom_call" | custom-call | bytes 60000000 | tf_op jit(solution)/shard_map/gather_tokens/pallas_call | solution.py:148
  233.0 6.4 copy.196
  247.8 10.8 %collective-permute-done.9 = bf16[256,1536]{1,0:T(8,128)(2,1)S(1)} collective-permute-done((bf16[256,1536]{1,0:T(8,128)(2,1)}, bf16[256,1536]{1,0:T(8,128)(2,1)S(1)}, u32[]{:S(2)}, u32[]{:S(2)}) %collective-permute-start.9) | collective-permute-done | bytes 786464 | tf_op jit(solution)/shard_map/ppermute | solution.py:448
  259.6 51.0 %collective-permute-done.10 = bf16[256,1536]{1,0:T(8,128)(2,1)S(1)} collective-permute-done((bf16[256,1536]{1,0:T(8,128)(2,1)}, bf16[256,1536]{1,0:T(8,128)(2,1)S(1)}, u32[]{:S(2)}, u32[]{:S(2)}) %collective-permute-start.10) | collective-permute-done | bytes 786464 | tf_op jit(solution)/shard_map/ppermute | solution.py:448
  315.2 4.7 fusion.2
  328.4 4.8 convolution_convert_fusion.3
  333.3 29.3 %scatter_sum.4 = f32[64,2048]{1,0:T(8,128)S(1)} custom-call(bf16[8,2,64,2048]{3,2,1,0:T(8,128)(2,1)S(1)} %bitcast.289), custom_call_target="tpu_custom_call" | custom-call | bytes 60000000 | tf_op jit(solution)/shard_map/scatter_sum/pallas_call | solution.py:202
  363.7 32.4 %gather_tokens.3 = bf16[8,2,64,2048]{3,2,1,0:T(8,128)(2,1)} custom-call(bf16[64,2048]{1,0:T(8,128)(2,1)} %fusion.103.refs_0_), custom_call_target="tpu_custom_call" | custom-call | bytes 60000000 | tf_op jit(solution)/shard_map/gather_tokens/pallas_call | solution.py:148
  414.8 6.4 attend_back.1
  423.0 26.7 %scatter_key_grads.1 = f32[1024,128]{1,0:T(8,128)} custom-call(bf16[4,1024,128]{2,1,0:T(8,128)(2,1)} %bitcast.293), custom_call_target="tpu_custom_call" | custom-call | bytes 30000000 | tf_op jit(solution)/shard_map/scatter_key_grads/pallas_call | solution.py:279
  452.4 6.4 copy.190
  473.9 7.0 %convolution_convert_fusion.4 = bf16[8,256,1024]{2,1,0:T(8,128)(2,1)} fusion(bf16[8,256,1024]{2,1,0:T(8,128)(2,1)S(1)} %bitcast.318, bf16[1024,512]{0,1:T(8,128)(2,1)S(1)} %copy-done.80, bf16[1024,512]{0,1:T(8,128)(2,1)S(1)} %copy-done.78), kind=kOutput, calls=%fused_computation.34 | convolution fusion | flops 4301258752 | bytes 10485760 | tf_op jit(solution)/shard_map/dot_general | solution.py:302
  481.0 6.5 copy.207
  511.3 40.0 %scatter_sum.5 = f32[64,2048]{1,0:T(8,128)S(1)} custom-call(bf16[8,2,64,2048]{3,2,1,0:T(8,128)(2,1)S(1)} %bitcast.287), custom_call_target="tpu_custom_call" | custom-call | bytes 60000000 | tf_op jit(solution)/shard_map/scatter_sum/pallas_call | solution.py:202
  566.9 57.4 %all-to-all-done.2 = bf16[8,32,384]{2,1,0:T(8,128)(2,1)} async-done(((bf16[8,32,384]{2,1,0:T(8,128)(2,1)}), bf16[8,32,384]{2,1,0:T(8,128)(2,1)}, u32[]{:S(2)}, u32[]{:S(2)}) %all-to-all-start.2) | async-done | bytes 196640 | tf_op jit(solution)/shard_map/all_to_all | solution.py:474
  645.0 10.4 %all-to-all-done.3 = bf16[8,32,1536]{2,1,0:T(8,128)(2,1)S(1)} async-done(((bf16[8,32,1536]{2,1,0:T(8,128)(2,1)}), bf16[8,32,1536]{2,1,0:T(8,128)(2,1)S(1)}, u32[]{:S(2)}, u32[]{:S(2)}) %all-to-all-start.3) | async-done | bytes 786464 | tf_op jit(solution)/shard_map/all_to_all | solution.py:474
  674.6 14.0 %collective-permute-start.46 = (f32[2,32]{1,0:T(2,128)S(1)}, f32[2,32]{1,0:T(2,128)S(1)}, u32[]{:S(2)}, u32[]{:S(2)}) collective-permute-start(f32[2,32]{1,0:T(2,128)S(1)} %pad_maximum_fusion.12), channel_id=1, source_target_pairs={{0,1},{1,0},{2,3},{3,2},{4,5},{5,4},{6,7},{7,6},{8,9},{9,8},{10,11... | collective-permute-start | bytes 776 | tf_op jit(solution)/shard_map/ppermute | solution.py:452
  689.3 6.9 collective-permute-start.31
  (415 shorter events, 231.6 us)
Async XLA Ops:
  3.1 74.8 %collective-permute-start.23 = (bf16[64,2048]{1,0:T(8,128)(2,1)S(1)}, bf16[64,2048]{1,0:T(8,128)(2,1)}, u32[]{:S(2)}, u32[]{:S(2)}) collective-permute-start(bf16[64,2048]{1,0:T(8,128)(2,1)S(1)} %get-tuple-element.116), channel_id=1, source_target_pairs={{0,2},{2,0},{4,6},{6,4},{8,10},{10,8},{12,14},{14,12},{1,3},{3,1},... | collective-permute-start | bytes 786440 | tf_op jit(solution)/shard_map/ppermute | solution.py:448
  5.2 77.0 %collective-permute-start.24 = (bf16[64,2048]{1,0:T(8,128)(2,1)S(1)}, bf16[64,2048]{1,0:T(8,128)(2,1)}, u32[]{:S(2)}, u32[]{:S(2)}) collective-permute-start(bf16[64,2048]{1,0:T(8,128)(2,1)S(1)} %get-tuple-element.116), channel_id=1, source_target_pairs={{0,4},{2,6},{4,8},{6,10},{8,12},{10,14},{12,0},{14,2},{1,5},{3,7},... | collective-permute-start | bytes 786440 | tf_op jit(solution)/shard_map/ppermute | solution.py:448
  6.9 78.5 %collective-permute-start.25 = (bf16[64,2048]{1,0:T(8,128)(2,1)S(1)}, bf16[64,2048]{1,0:T(8,128)(2,1)}, u32[]{:S(2)}, u32[]{:S(2)}) collective-permute-start(bf16[64,2048]{1,0:T(8,128)(2,1)S(1)} %get-tuple-element.116), channel_id=1, source_target_pairs={{0,6},{2,4},{4,10},{6,8},{8,14},{10,12},{12,2},{14,0},{1,7},{3,5},... | collective-permute-start | bytes 786440 | tf_op jit(solution)/shard_map/ppermute | solution.py:448
  8.4 79.8 %collective-permute-start.26 = (bf16[64,2048]{1,0:T(8,128)(2,1)S(1)}, bf16[64,2048]{1,0:T(8,128)(2,1)}, u32[]{:S(2)}, u32[]{:S(2)}) collective-permute-start(bf16[64,2048]{1,0:T(8,128)(2,1)S(1)} %get-tuple-element.116), channel_id=1, source_target_pairs={{0,8},{2,10},{4,12},{6,14},{8,0},{10,2},{12,4},{14,6},{1,9},{3,11}... | collective-permute-start | bytes 786440 | tf_op jit(solution)/shard_map/ppermute | solution.py:448
  10.2 82.2 %collective-permute-start.27 = (bf16[64,2048]{1,0:T(8,128)(2,1)S(1)}, bf16[64,2048]{1,0:T(8,128)(2,1)}, u32[]{:S(2)}, u32[]{:S(2)}) collective-permute-start(bf16[64,2048]{1,0:T(8,128)(2,1)S(1)} %get-tuple-element.116), channel_id=1, source_target_pairs={{0,10},{2,8},{4,14},{6,12},{8,2},{10,0},{12,6},{14,4},{1,11},{3,9}... | collective-permute-start | bytes 786440 | tf_op jit(solution)/shard_map/ppermute | solution.py:448
  13.8 59.7 %all-to-all-start = ((bf16[8,32,384]{2,1,0:T(8,128)(2,1)}), bf16[8,32,384]{2,1,0:T(8,128)(2,1)S(1)}, u32[]{:S(2)}, u32[]{:S(2)}) async-start(bf16[8,32,384]{2,1,0:T(8,128)(2,1)} %copy.171), calls=%async_computation | async-start | bytes 393216 | tf_op jit(solution)/shard_map/all_to_all | solution.py:474
  73.5 108.7 %all-to-all-start.1 = ((bf16[8,32,1536]{2,1,0:T(8,128)(2,1)}), bf16[8,32,1536]{2,1,0:T(8,128)(2,1)}, u32[]{:S(2)}, u32[]{:S(2)}) async-start(bf16[8,32,1536]{2,1,0:T(8,128)(2,1)} %copy.178), calls=%async_computation.1 | async-start | bytes 1572864 | tf_op jit(solution)/shard_map/all_to_all | solution.py:474
  111.2 208.7 %collective-permute-start.30 = (bf16[8,64,2048]{2,1,0:T(8,128)(2,1)}, bf16[8,64,2048]{2,1,0:T(8,128)(2,1)}, u32[]{:S(2)}, u32[]{:S(2)}) collective-permute-start(bf16[8,64,2048]{2,1,0:T(8,128)(2,1)} %bitcast_dynamic-update-slice_fusion.8), channel_id=1, source_target_pairs={{0,1},{1,0},{2,3},{3,2},{4,5},{5,4},{6,7},{7,6},{8,9},{9,8},{10,11... | collective-permute-start | bytes 6291464 | tf_op jit(solution)/shard_map/ppermute | solution.py:452
  182.2 58.9 %collective-permute-start.7 = (bf16[256,1536]{1,0:T(8,128)(2,1)}, bf16[256,1536]{1,0:T(8,128)(2,1)}, u32[]{:S(2)}, u32[]{:S(2)}) collective-permute-start(bf16[256,1536]{1,0:T(8,128)(2,1)} %bitcast.42), channel_id=1, source_target_pairs={{0,16},{16,32},{32,48},{48,0},{64,80},{80,96},{96,112},{112,64},{1... | collective-permute-start | bytes 2359304 | tf_op jit(solution)/shard_map/ppermute | solution.py:448
  182.8 63.7 %collective-permute-start.8 = (bf16[256,1536]{1,0:T(8,128)(2,1)}, bf16[256,1536]{1,0:T(8,128)(2,1)}, u32[]{:S(2)}, u32[]{:S(2)}) collective-permute-start(bf16[256,1536]{1,0:T(8,128)(2,1)} %bitcast.42), channel_id=1, source_target_pairs={{0,32},{16,48},{32,0},{48,16},{64,96},{80,112},{96,64},{112,80},{1... | collective-permute-start | bytes 2359304 | tf_op jit(solution)/shard_map/ppermute | solution.py:448
  239.4 71.3 %collective-permute-start.10 = (bf16[256,1536]{1,0:T(8,128)(2,1)}, bf16[256,1536]{1,0:T(8,128)(2,1)S(1)}, u32[]{:S(2)}, u32[]{:S(2)}) collective-permute-start(bf16[256,1536]{1,0:T(8,128)(2,1)} %bitcast.42), channel_id=1, source_target_pairs={{0,64},{16,80},{32,96},{48,112},{64,0},{80,16},{96,32},{112,48},{1... | collective-permute-start | bytes 2359304 | tf_op jit(solution)/shard_map/ppermute | solution.py:448
  241.1 69.6 %collective-permute-start.11 = (bf16[256,1536]{1,0:T(8,128)(2,1)}, bf16[256,1536]{1,0:T(8,128)(2,1)S(1)}, u32[]{:S(2)}, u32[]{:S(2)}) collective-permute-start(bf16[256,1536]{1,0:T(8,128)(2,1)} %bitcast.42), channel_id=1, source_target_pairs={{0,80},{16,96},{32,112},{48,64},{64,16},{80,32},{96,48},{112,0},{1... | collective-permute-start | bytes 2359304 | tf_op jit(solution)/shard_map/ppermute | solution.py:448
  246.5 64.3 %collective-permute-start.12 = (bf16[256,1536]{1,0:T(8,128)(2,1)}, bf16[256,1536]{1,0:T(8,128)(2,1)S(1)}, u32[]{:S(2)}, u32[]{:S(2)}) collective-permute-start(bf16[256,1536]{1,0:T(8,128)(2,1)} %bitcast.42), channel_id=1, source_target_pairs={{0,96},{16,112},{32,64},{48,80},{64,32},{80,48},{96,0},{112,16},{1... | collective-permute-start | bytes 2359304 | tf_op jit(solution)/shard_map/ppermute | solution.py:448
  258.6 52.3 %collective-permute-start.13 = (bf16[256,1536]{1,0:T(8,128)(2,1)}, bf16[256,1536]{1,0:T(8,128)(2,1)S(1)}, u32[]{:S(2)}, u32[]{:S(2)}) collective-permute-start(bf16[256,1536]{1,0:T(8,128)(2,1)} %bitcast.42), channel_id=1, source_target_pairs={{0,112},{16,64},{32,80},{48,96},{64,48},{80,0},{96,16},{112,32},{1... | collective-permute-start | bytes 2359304 | tf_op jit(solution)/shard_map/ppermute | solution.py:448
  499.5 61.8 %collective-permute-start.39 = (bf16[256,1536]{1,0:T(8,128)(2,1)}, bf16[256,1536]{1,0:T(8,128)(2,1)}, u32[]{:S(2)}, u32[]{:S(2)}) collective-permute-start(bf16[256,1536]{1,0:T(8,128)(2,1)} %get-tuple-element.83), channel_id=1, source_target_pairs={{0,16},{16,32},{32,48},{48,0},{64,80},{80,96},{96,112},{112,64},{1... | collective-permute-start | bytes 2359304 | tf_op jit(solution)/shard_map/ppermute | solution.py:448
  500.0 62.8 %collective-permute-start.40 = (bf16[256,1536]{1,0:T(8,128)(2,1)}, bf16[256,1536]{1,0:T(8,128)(2,1)}, u32[]{:S(2)}, u32[]{:S(2)}) collective-permute-start(bf16[256,1536]{1,0:T(8,128)(2,1)} %get-tuple-element.84), channel_id=1, source_target_pairs={{0,32},{16,48},{32,0},{48,16},{64,96},{80,112},{96,64},{112,80},{1... | collective-permute-start | bytes 2359304 | tf_op jit(solution)/shard_map/ppermute | solution.py:448
  504.6 46.9 %collective-permute-start.37 = (bf16[256,384]{0,1:T(8,128)(2,1)S(1)}, bf16[256,384]{0,1:T(8,128)(2,1)S(1)}, u32[]{:S(2)}, u32[]{:S(2)}) collective-permute-start(bf16[256,384]{0,1:T(8,128)(2,1)S(1)} %copy-done.54), channel_id=1, source_target_pairs={{0,96},{16,112},{32,64},{48,80},{64,32},{80,48},{96,0},{112,16},{1... | collective-permute-start | bytes 589832 | tf_op jit(solution)/shard_map/ppermute | solution.py:448
  504.7 46.9 %collective-permute-start.38 = (bf16[256,384]{0,1:T(8,128)(2,1)S(1)}, bf16[256,384]{0,1:T(8,128)(2,1)S(1)}, u32[]{:S(2)}, u32[]{:S(2)}) collective-permute-start(bf16[256,384]{0,1:T(8,128)(2,1)S(1)} %fusion.83), channel_id=1, source_target_pairs={{0,112},{16,64},{32,80},{48,96},{64,48},{80,0},{96,16},{112,32},{1... | collective-permute-start | bytes 589832 | tf_op jit(solution)/shard_map/ppermute | solution.py:448
  509.4 119.8 %collective-permute-start.41 = (bf16[256,1536]{1,0:T(8,128)(2,1)}, bf16[256,1536]{1,0:T(8,128)(2,1)}, u32[]{:S(2)}, u32[]{:S(2)}) collective-permute-start(bf16[256,1536]{1,0:T(8,128)(2,1)} %get-tuple-element.85), channel_id=1, source_target_pairs={{0,48},{16,0},{32,16},{48,32},{64,112},{80,64},{96,80},{112,96},{1... | collective-permute-start | bytes 2359304 | tf_op jit(solution)/shard_map/ppermute | solution.py:448
  551.5 82.7 %collective-permute-start.42 = (bf16[256,1536]{1,0:T(8,128)(2,1)}, bf16[256,1536]{1,0:T(8,128)(2,1)}, u32[]{:S(2)}, u32[]{:S(2)}) collective-permute-start(bf16[256,1536]{1,0:T(8,128)(2,1)} %get-tuple-element.86), channel_id=1, source_target_pairs={{0,64},{16,80},{32,96},{48,112},{64,0},{80,16},{96,32},{112,48},{1... | collective-permute-start | bytes 2359304 | tf_op jit(solution)/shard_map/ppermute | solution.py:448
  551.6 82.6 %collective-permute-start.43 = (bf16[256,1536]{1,0:T(8,128)(2,1)}, bf16[256,1536]{1,0:T(8,128)(2,1)}, u32[]{:S(2)}, u32[]{:S(2)}) collective-permute-start(bf16[256,1536]{1,0:T(8,128)(2,1)} %get-tuple-element.87), channel_id=1, source_target_pairs={{0,80},{16,96},{32,112},{48,64},{64,16},{80,32},{96,48},{112,0},{1... | collective-permute-start | bytes 2359304 | tf_op jit(solution)/shard_map/ppermute | solution.py:448
  556.8 67.6 %all-to-all-start.2 = ((bf16[8,32,384]{2,1,0:T(8,128)(2,1)}), bf16[8,32,384]{2,1,0:T(8,128)(2,1)}, u32[]{:S(2)}, u32[]{:S(2)}) async-start(bf16[8,32,384]{2,1,0:T(8,128)(2,1)} %bitcast.356), calls=%async_computation.2 | async-start | bytes 393216 | tf_op jit(solution)/shard_map/all_to_all | solution.py:474
  561.4 72.9 %collective-permute-start.44 = (bf16[256,1536]{1,0:T(8,128)(2,1)}, bf16[256,1536]{1,0:T(8,128)(2,1)}, u32[]{:S(2)}, u32[]{:S(2)}) collective-permute-start(bf16[256,1536]{1,0:T(8,128)(2,1)} %get-tuple-element.88), channel_id=1, source_target_pairs={{0,96},{16,112},{32,64},{48,80},{64,32},{80,48},{96,0},{112,16},{1... | collective-permute-start | bytes 2359304 | tf_op jit(solution)/shard_map/ppermute | solution.py:448
  562.8 71.4 %collective-permute-start.45 = (bf16[256,1536]{1,0:T(8,128)(2,1)}, bf16[256,1536]{1,0:T(8,128)(2,1)}, u32[]{:S(2)}, u32[]{:S(2)}) collective-permute-start(bf16[256,1536]{1,0:T(8,128)(2,1)} %fusion.34), channel_id=1, source_target_pairs={{0,112},{16,64},{32,80},{48,96},{64,48},{80,0},{96,16},{112,32},{1... | collective-permute-start | bytes 2359304 | tf_op jit(solution)/shard_map/ppermute | solution.py:448
  (108 other events, 2210.0 us)

commit v2 on v1

--- a/solution.py
+++ b/solution.py
@@ -74,100 +74,78 @@
     )
 
 
-def gather_kernel(with_segments, *refs):
-    if with_segments:
-        x_ref, seg_ref, out_ref, seg_out, send, recv, tsend, trecv, local, ssend, srecv, xsend, xrecv, slocal = refs
-    else:
-        x_ref, out_ref, send, recv, tsend, trecv, local = refs
-    t = lax.axis_index("t")
-    moves = shifts(GROUP)[1:]
-    crossings = [(s,) for s in (1, 2, 3)]
-    devices = [other_core()] + [peer(GROUP, s) for s in moves]
-    if with_segments:
-        devices = devices + [peer(("x",), s) for s in crossings]
-    greet(devices)
-    me = place(GROUP, (0, 0))
-    copies = []
+DMA = pltpu.SemaphoreType.DMA
+HBM = pl.BlockSpec(memory_space=pl.ANY)
+VMEM = pl.BlockSpec(memory_space=pltpu.VMEM)
+MOVES = shifts(GROUP)[1:]
+TURNS = (1, 3, 2)
+
+
+def members():
+    return [other_core()] + [peer(GROUP, s) for s in MOVES]
+
+
+def across():
+    return [peer(("dp",), (1,))] + [peer(("x",), (s,)) for s in TURNS]
+
+
+def finish(copies):
+    for c in copies:
+        c.wait()
+
+
+GATHER_SEMS = [DMA((7,)), DMA((7,)), DMA((8,)), DMA((8,)), DMA]
+
+
+def gather_start(x_ref, out_ref, sems):
+    send, recv, tsend, trecv, local = sems
+    t, me = lax.axis_index("t"), place(GROUP, (0, 0))
     own = pltpu.make_async_copy(x_ref, out_ref.at[me, t], local)
     own.start()
-    if with_segments:
-        x = lax.axis_index("x")
-        seg_own = pltpu.make_async_copy(seg_ref, seg_out.at[x, me], slocal)
-        seg_own.start()
-        seg_copies = []
-        for i, s in enumerate(moves):
-            c = remote(seg_ref, seg_out.at[x, me], ssend.at[i], srecv.at[i], peer(GROUP, s))
-            c.start()
-            seg_copies.append(c)
-    for i, s in enumerate(moves):
+    copies = []
+    for i, s in enumerate(MOVES):
         c = remote(x_ref, out_ref.at[me, t], send.at[i], recv.at[i], peer(GROUP, s))
         c.start()
         copies.append(c)
     c = remote(x_ref, out_ref.at[me, t], tsend.at[7], trecv.at[7], other_core())
     c.start()
-    passed = [c]
-    if with_segments:
-        seg_own.wait()
-        for c in seg_copies:
-            c.wait()
-        crossed = []
-        for i, s in enumerate(crossings):
-            c = remote(seg_out.at[x], seg_out.at[x], xsend.at[i], xrecv.at[i], peer(("x",), s))
-            c.start()
-            crossed.append(c)
-    for i, s in enumerate(moves):
+    return own, copies, [c]
+
+
+def gather_finish(state, out_ref, sems):
+    own, copies, passed = state
+    _, _, tsend, trecv, _ = sems
+    t = lax.axis_index("t")
+    for i, s in enumerate(MOVES):
         copies[i].wait_recv()
-        source = place(GROUP, s, -1)
-        c = remote(
-            out_ref.at[source, t], out_ref.at[source, t], tsend.at[i], trecv.at[i], other_core()
-        )
+        part = out_ref.at[place(GROUP, s, -1), t]
+        c = remote(part, part, tsend.at[i], trecv.at[i], other_core())
         c.start()
         passed.append(c)
     own.wait()
     for c in copies:
         c.wait_send()
-    for c in passed:
-        c.wait()
-    if with_segments:
-        for c in crossed:
-            c.wait()
-
-
-def gather_tokens(x, segments=None):
-    with_segments = segments is not None
-    wide = x.shape[1]
-    dma = pltpu.SemaphoreType.DMA
-    out_shape = [jax.ShapeDtypeStruct((MEMBERS, 2, HALF, wide), x.dtype)]
-    scratch = [dma((7,)), dma((7,)), dma((8,)), dma((8,)), dma]
-    args = [x]
-    if with_segments:
-        out_shape.append(jax.ShapeDtypeStruct((4, MEMBERS, 8, 128), jnp.int32))
-        scratch = scratch + [dma((7,)), dma((7,)), dma((3,)), dma((3,)), dma]
-        args.append(segments)
-    hbm = pl.BlockSpec(memory_space=pl.ANY)
-    out = pl.pallas_call(
-        functools.partial(gather_kernel, with_segments),
-        out_shape=out_shape,
-        in_specs=[hbm] * len(args),
-        out_specs=[hbm] * len(out_shape),
-        scratch_shapes=scratch,
-        compiler_params=pltpu.CompilerParams(
-            collective_id=1 if with_segments else 2, has_side_effects=True
-        ),
-        cost_estimate=pl.CostEstimate(flops=0, bytes_accessed=60_000_000, transcendentals=0),
-        name="gather_tokens_first" if with_segments else "gather_tokens",
-    )(*args)
-    gathered = out[0].reshape(ROWS, wide)
-    return (gathered, out[1]) if with_segments else gathered
-
-
-def scatter_kernel(p_ref, out_ref, mine, theirs, sums, land, lsem, tsend, trecv, send, recv):
+    finish(passed)
+
+
+SCATTER_SEMS = [DMA((8,)), DMA((8,)), DMA((8,)), DMA((7,)), DMA((7,))]
+
+
+def scatter_slots(wide):
+    return [
+        pltpu.VMEM((MEMBERS, HALF, wide), BF),
+        pltpu.VMEM((MEMBERS, HALF, wide), BF),
+        pltpu.VMEM((7, HALF, wide), BF),
+        pltpu.VMEM((7, HALF, wide), BF),
+    ]
+
+
+def scatter_start(p_ref, slots, sems):
+    mine, theirs, _, _ = slots
+    lsem, tsend, trecv, _, _ = sems
     t = lax.axis_index("t")
-    moves = shifts(GROUP)
-    order = moves[1:] + moves[:1]
-    greet([other_core()] + [peer(GROUP, s) for s in moves[1:]])
     loads, swaps = [], []
-    for i, s in enumerate(order):
+    for i, s in enumerate(MOVES + [(0, 0)]):
         chunk = place(GROUP, s)
         c = remote(p_ref.at[chunk, 1 - t], theirs.at[i], tsend.at[i], trecv.at[i], other_core())
         c.start()
@@ -175,8 +153,15 @@
         c = pltpu.make_async_copy(p_ref.at[chunk, t], mine.at[i], lsem.at[i])
         c.start()
         loads.append(c)
+    return loads, swaps
+
+
+def scatter_send(state, slots, sems):
+    loads, swaps = state
+    mine, theirs, sums, land = slots
+    _, _, _, send, recv = sems
     copies = []
-    for i, s in enumerate(order[:7]):
+    for i, s in enumerate(MOVES):
         loads[i].wait()
         swaps[i].wait_recv()
         sums[i] = (mine[i].astype(F32) + theirs[i].astype(F32)).astype(BF)
@@ -185,113 +170,453 @@
         copies.append(c)
     loads[7].wait()
     swaps[7].wait_recv()
-    out_ref[...] = mine[7].astype(F32) + theirs[7].astype(F32)
+    return copies
+
+
+def scatter_total(state, copies, slots, total):
+    _, swaps = state
+    mine, theirs, _, land = slots
+    total[...] = mine[7].astype(F32) + theirs[7].astype(F32)
     for i in range(7):
         copies[i].wait_recv()
-        out_ref[...] += land[i].astype(F32)
+        total[...] += land[i].astype(F32)
+    for c in copies + swaps:
+        c.wait_send()
+
+
+SPREAD_SEMS = [DMA((7,)), DMA((7,)), DMA]
+
+
+def spread_start(x_ref, out_ref, sems):
+    send, recv, local = sems
+    dp, x = lax.axis_index("dp"), lax.axis_index("x")
+    own = pltpu.make_async_copy(x_ref, out_ref.at[dp, x], local)
+    own.start()
+    copies = []
+    for i, to in enumerate(across()):
+        c = remote(x_ref, out_ref.at[dp, x], send.at[i], recv.at[i], to)
+        c.start()
+        copies.append(c)
+    return own, copies
+
+
+def spread_pass(state, out_ref, sems):
+    _, copies = state
+    send, recv, _ = sems
+    part = out_ref.at[1 - lax.axis_index("dp"), lax.axis_index("x")]
+    copies[0].wait_recv()
+    for i, to in enumerate(across()[1:]):
+        c = remote(part, part, send.at[4 + i], recv.at[4 + i], to)
+        c.start()
+        copies.append(c)
+
+
+def spread_finish(state):
+    own, copies = state
+    own.wait()
+    copies[0].wait_send()
+    finish(copies[1:])
+
+
+REDUCE_SEMS = [DMA((2,)), DMA((7,)), DMA((7,))]
+
+
+def reduce_slots(wide):
+    return [
+        pltpu.VMEM((2, 256, wide), BF),
+        pltpu.VMEM((6, 256, wide), BF),
+        pltpu.VMEM((256, wide), BF),
+        pltpu.VMEM((256, wide), BF),
+    ]
+
+
+def reduce_start(p_ref, slots, sems):
+    mine, land, _, _ = slots
+    lsem, send, recv = sems
+    dp, x = lax.axis_index("dp"), lax.axis_index("x")
+    loads, copies = [], []
+    for j, row in enumerate((1 - dp, dp)):
+        c = pltpu.make_async_copy(p_ref.at[row, x], mine.at[j], lsem.at[j])
+        c.start()
+        loads.append(c)
+        for i, s in enumerate(TURNS):
+            k = 3 * j + i
+            c = remote(
+                p_ref.at[row, place(("x",), (s,))],
+                land.at[k],
+                send.at[k],
+                recv.at[k],
+                peer(("x",), (s,)),
+            )
+            c.start()
+            copies.append(c)
+    return loads, copies
+
+
+def add_rows(out_ref, terms):
+    rows = 32
+
+    def step(r, carry):
+        at = pl.ds(pl.multiple_of(r * rows, rows), rows)
+        total = terms[0][at, :].astype(F32)
+        for term in terms[1:]:
+            total = total + term[at, :].astype(F32)
+        out_ref[at, :] = total.astype(out_ref.dtype)
+        return carry
+
+    lax.fori_loop(0, 256 // rows, step, 0)
+
+
+def reduce_pass(state, slots, sems):
+    loads, copies = state
+    mine, land, fold, back = slots
+    _, send, recv = sems
+    loads[0].wait()
+    for c in copies[:3]:
+        c.wait_recv()
+    add_rows(fold, [mine.at[0]] + [land.at[i] for i in range(3)])
+    c = remote(fold, back, send.at[6], recv.at[6], peer(("dp",), (1,)))
+    c.start()
+    copies.append(c)
+
+
+def reduce_total(state, slots, out_ref):
+    loads, copies = state
+    mine, land, _, back = slots
+    loads[1].wait()
+    for c in copies[3:]:
+        c.wait_recv()
+    add_rows(out_ref, [mine.at[1], back] + [land.at[3 + i] for i in range(3)])
     for c in copies:
         c.wait_send()
-    for c in swaps:
-        c.wait_send()
-
-
-def scatter_sum(partial_sum):
-    wide = partial_sum.shape[1]
-    dma = pltpu.SemaphoreType.DMA
-    slots = (MEMBERS, HALF, wide)
-    return pl.pallas_call(
-        scatter_kernel,
-        out_shape=jax.ShapeDtypeStruct((HALF, wide), F32),
-        in_specs=[pl.BlockSpec(memory_space=pl.ANY)],
-        out_specs=pl.BlockSpec(memory_space=pltpu.VMEM),
-        scratch_shapes=[
-            pltpu.VMEM(slots, BF),
-            pltpu.VMEM(slots, BF),
-            pltpu.VMEM((7, HALF, wide), BF),
-            pltpu.VMEM((7, HALF, wide), BF),
-            dma((8,)),
-            dma((8,)),
-            dma((8,)),
-            dma((7,)),
-            dma((7,)),
-        ],
-        compiler_params=pltpu.CompilerParams(
-            collective_id=3, has_side_effects=True, vmem_limit_bytes=32 * 2**20
-        ),
-        cost_estimate=pl.CostEstimate(flops=0, bytes_accessed=60_000_000, transcendentals=0),
-        name="scatter_sum",
-    )(partial_sum.reshape(MEMBERS, 2, HALF, wide))
-
-
-def gather_x_kernel(x_ref, out_ref, send, recv, local):
-    moves = [(s,) for s in (1, 2, 3)]
-    greet([peer(("x",), s) for s in moves])
-    me = lax.axis_index("x")
-    own = pltpu.make_async_copy(x_ref, out_ref.at[me], local)
+
+
+DEAL_SEMS = [DMA((7,)), DMA((7,)), DMA]
+
+
+def deal_start(x_ref, out_ref, sems):
+    send, recv, local = sems
+    me = place(GROUP, (0, 0))
+    own = pltpu.make_async_copy(x_ref.at[me], out_ref.at[me], local)
     own.start()
     copies = []
-    for i, s in enumerate(moves):
-        c = remote(x_ref, out_ref.at[me], send.at[i], recv.at[i], peer(("x",), s))
+    for i, s in enumerate(MOVES):
+        c = remote(
+            x_ref.at[place(GROUP, s)], out_ref.at[me], send.at[i], recv.at[i], peer(GROUP, s)
+        )
         c.start()
         copies.append(c)
-    own.wait()
+    return [own] + copies
+
+
+def split(refs, *counts):
+    parts, at = [], 0
+    for count in counts:
+        parts.append(refs[at : at + count])
+        at += count
+    assert at == len(refs)
+    return parts
+
+
+def scale_rows(x):
+    return lax.rsqrt(jnp.mean(x * x, axis=1, keepdims=True) + EPS)
+
+
+def norm_back(unit, inverse, grad):
+    return inverse * (grad - unit * jnp.mean(grad * unit, axis=1, keepdims=True))
+
+
+def call(kernel, collective_id, name, args, in_specs, outs, out_specs, scratch):
+    sent = 60_000_000
+    return pl.pallas_call(
+        kernel,
+        out_shape=[jax.ShapeDtypeStruct(s, d) for s, d in outs],
+        in_specs=in_specs,
+        out_specs=out_specs,
+        scratch_shapes=scratch,
+        compiler_params=pltpu.CompilerParams(
+            collective_id=collective_id, has_side_effects=True, vmem_limit_bytes=56 * 2**20
+        ),
+        cost_estimate=pl.CostEstimate(flops=0, bytes_accessed=sent, transcendentals=0),
+        name=name,
+    )(*args)
+
+
+def first_kernel(*refs):
+    ins, outs, dealt, gather, deal_a, deal_b, spread_a, spread_b, seg_sems = split(
+        refs, 4, 4, 2, 5, 3, 3, 3, 3, 5
+    )
+    x_ref, seg_ref, qkv_ref, wo_ref = ins
+    all_ref, seg_out, w_qkv, w_out = outs
+    part_a, part_b = dealt
+    ssend, srecv, xsend, xrecv, slocal = seg_sems
+    greet(members() + across())
+    deals = deal_start(qkv_ref, part_a, deal_a) + deal_start(wo_ref, part_b, deal_b)
+    me, x = place(GROUP, (0, 0)), lax.axis_index("x")
+    seg_own = pltpu.make_async_copy(seg_ref, seg_out.at[x, me], slocal)
+    seg_own.start()
+    seg_copies = [seg_own]
+    for i, s in enumerate(MOVES):
+        c = remote(seg_ref, seg_out.at[x, me], ssend.at[i], srecv.at[i], peer(GROUP, s))
+        c.start()
+        seg_copies.append(c)
+    tokens = gather_start(x_ref, all_ref, gather)
+    finish(deals)
+    spreads = [spread_start(part_a, w_qkv, spread_a), spread_start(part_b, w_out, spread_b)]
+    finish(seg_copies)
+    crossed = []
+    for i, to in enumerate(across()[1:]):
+        c = remote(seg_out.at[x], seg_out.at[x], xsend.at[i], xrecv.at[i], to)
+        c.start()
+        crossed.append(c)
+    spread_pass(spreads[0], w_qkv, spread_a)
+    spread_pass(spreads[1], w_out, spread_b)
+    gather_finish(tokens, all_ref, gather)
+    for s in spreads:
+        spread_finish(s)
+    finish(crossed)
+
+
+def first_exchange(unit, segments, qkv_slots, out_slots):
+    outs = [
+        ((MEMBERS, 2, HALF, D), BF),
+        ((4, MEMBERS, 8, 128), jnp.int32),
+        ((2, 4, MEMBERS, 32, 256), BF),
+        ((2, 4, MEMBERS, 32, 128), BF),
+    ]
+    scratch = [pltpu.VMEM((MEMBERS, 32, 256), BF), pltpu.VMEM((MEMBERS, 32, 128), BF)]
+    scratch += GATHER_SEMS + DEAL_SEMS * 2 + SPREAD_SEMS * 2
+    scratch += [DMA((7,)), DMA((7,)), DMA((3,)), DMA((3,)), DMA]
+    args = (unit, segments, qkv_slots, out_slots)
+    tokens, seg, w_qkv, w_out = call(
+        first_kernel, 1, "first_exchange", args, [HBM] * 4, outs, [HBM] * 4, scratch
+    )
+    return tokens.reshape(ROWS, D), seg, w_qkv.reshape(D, 256), w_out.reshape(D, 128)
+
+
+def keys_kernel(*refs):
+    ins, outs, sems, deal_a, deal_b = split(refs, 3, 3, 3, 3, 3)
+    kv_ref, gu_ref, down_ref = ins
+    out_ref, gu_part, down_part = outs
+    send, recv, local = sems
+    greet(members()[1:] + across()[1:])
+    x = lax.axis_index("x")
+    copies = [pltpu.make_async_copy(kv_ref, out_ref.at[x], local)]
+    copies[0].start()
+    for i, to in enumerate(across()[1:]):
+        c = remote(kv_ref, out_ref.at[x], send.at[i], recv.at[i], to)
+        c.start()
+        copies.append(c)
+    copies = copies + deal_start(gu_ref, gu_part, deal_a) + deal_start(down_ref, down_part, deal_b)
+    finish(copies)
+
+
+def exchange_keys(kv, gate_up_slots, down_slots):
+    outs = [
+        ((4, ROWS, 128), BF),
+        ((MEMBERS, 32, 1024), BF),
+        ((MEMBERS, 32, 512), BF),
+    ]
+    scratch = [DMA((3,)), DMA((3,)), DMA] + DEAL_SEMS * 2
+    args = (kv, gate_up_slots, down_slots)
+    kv, gate_up, down = call(
+        keys_kernel, 2, "exchange_keys", args, [HBM] * 3, outs, [HBM] * 3, scratch
+    )
+    return kv.reshape(LENGTH, 128), gate_up, down
+
+
+def forward_kernel(*refs):
+    ins, outs, buffers, scatter_sems, gather, gather_b, spread_a, spread_b = split(
+        refs, 5, 5, 6, 5, 5, 5, 3, 3
+    )
+    p_ref, rows_ref, cot_ref, gu_ref, down_ref = ins
+    resid_ref, all_m, all_g, w_gu, w_down = outs
+    *scatter, total, unit = buffers
+    greet(members() + across())
+    partial_sums = scatter_start(p_ref, scatter, scatter_sems)
+    spreads = [spread_start(gu_ref, w_gu, spread_a), spread_start(down_ref, w_down, spread_b)]
+    sent = scatter_send(partial_sums, scatter, scatter_sems)
+    spread_pass(spreads[0], w_gu, spread_a)
+    scatter_total(partial_sums, sent, scatter, total)
+    resid = rows_ref[...] + total[...]
+    resid_ref[...] = resid
+    unit[...] = (resid * scale_rows(resid)).astype(BF)
+    tokens = gather_start(unit, all_m, gather)
+    cots = gather_start(cot_ref, all_g, gather_b)
+    spread_pass(spreads[1], w_down, spread_b)
+    gather_finish(tokens, all_m, gather)
+    gather_finish(cots, all_g, gather_b)
+    for s in spreads:
+        spread_finish(s)
+
+
+def forward_exchange(p, rows, cot, gate_up_part, down_part):
+    slots = (MEMBERS, 2, HALF, D)
+    outs = [
+        ((HALF, D), F32),
+        (slots, BF),
+        (slots, BF),
+        ((2, 4, MEMBERS, 32, 1024), BF),
+        ((2, 4, MEMBERS, 32, 512), BF),
+    ]
+    scratch = scatter_slots(D) + [pltpu.VMEM((HALF, D), F32), pltpu.VMEM((HALF, D), BF)]
+    scratch += SCATTER_SEMS + GATHER_SEMS * 2 + SPREAD_SEMS * 2
+    args = (p.reshape(slots), rows, cot, gate_up_part, down_part)
+    resid, all_m, all_g, w_gu, w_down = call(
+        forward_kernel,
+        3,
+        "forward_exchange",
+        args,
+        [HBM, VMEM, HBM, HBM, HBM],
+        outs,
+        [VMEM] + [HBM] * 4,
+        scratch,
+    )
+    return (
+        resid,
+        all_m.reshape(ROWS, D),
+        all_g.reshape(ROWS, D),
+        w_gu.reshape(D, 1024),
+        w_down.reshape(D, 512),
+    )
+
+
+def backward_kernel(*refs):
+    ins, outs, slots_a, slots_b, slots_c, others, sems_a, sems_b, sems_c, gather, osems = split(
+        refs, 5, 4, 4, 4, 4, 3, 5, 5, 3, 5, 3
+    )
+    pm_ref, pd_ref, resid_ref, cot_ref, mg_ref = ins
+    g_resid, all_r, block_out, m_sum = outs
+    total, low, out_low = others
+    greet(members() + across())
+    t = lax.axis_index("t")
+    state_a = scatter_start(pm_ref, slots_a, sems_a)
+    state_c = reduce_start(mg_ref, slots_c, sems_c)
+    sent_a = scatter_send(state_a, slots_a, sems_a)
+    state_b = scatter_start(pd_ref, slots_b, sems_b)
+    scatter_total(state_a, sent_a, slots_a, total)
+    resid = resid_ref[...]
+    inverse = scale_rows(resid)
+    grad = cot_ref[...].astype(F32) + norm_back(resid * inverse, inverse, total[...])
+    g_resid[...] = grad
+    low[...] = grad.astype(BF)
+    tokens = gather_start(low, all_r, gather)
+    sent_b = scatter_send(state_b, slots_b, sems_b)
+    reduce_pass(state_c, slots_c, sems_c)
+    gather_finish(tokens, all_r, gather)
+    scatter_total(state_b, sent_b, slots_b, total)
+    out_low[...] = (resid_ref[...] + total[...]).astype(BF)
+    osend, orecv, local = osems
+    copies = [
+        pltpu.make_async_copy(out_low, block_out.at[t], local),
+        remote(out_low, block_out.at[t], osend, orecv, other_core()),
+    ]
     for c in copies:
-        c.wait()
-
-
-def gather_x(x):
-    dma = pltpu.SemaphoreType.DMA
-    hbm = pl.BlockSpec(memory_space=pl.ANY)
-    out = pl.pallas_call(
-        gather_x_kernel,
-        out_shape=jax.ShapeDtypeStruct((4,) + x.shape, x.dtype),
-        in_specs=[hbm],
-        out_specs=hbm,
-        scratch_shapes=[dma((3,)), dma((3,)), dma],
-        compiler_params=pltpu.CompilerParams(collective_id=4, has_side_effects=True),
-        cost_estimate=pl.CostEstimate(flops=0, bytes_accessed=30_000_000, transcendentals=0),
-        name="gather_keys",
-    )(x)
-    return out.reshape(4 * x.shape[0], x.shape[1])
-
-
-def scatter_x_kernel(p_ref, out_ref, mine, land, lsem, send, recv):
-    moves = [(s,) for s in (1, 2, 3)]
-    greet([peer(("x",), s) for s in moves])
-    me = lax.axis_index("x")
-    own = pltpu.make_async_copy(p_ref.at[me], mine, lsem)
+        c.start()
+    reduce_total(state_c, slots_c, m_sum)
+    finish(copies)
+
+
+def backward_exchange(pm, pd, resid, cot, grads):
+    slots = (MEMBERS, 2, HALF, D)
+    outs = [
+        ((HALF, D), F32),
+        (slots, BF),
+        ((2, HALF, D), BF),
+        ((256, 1536), BF),
+    ]
+    scratch = scatter_slots(D) * 2 + reduce_slots(1536)
+    scratch += [pltpu.VMEM((HALF, D), F32), pltpu.VMEM((HALF, D), BF), pltpu.VMEM((HALF, D), BF)]
+    scratch += SCATTER_SEMS * 2 + REDUCE_SEMS + GATHER_SEMS + [DMA, DMA, DMA]
+    args = (pm.reshape(slots), pd.reshape(slots), resid, cot, grads.reshape(2, 4, 256, 1536))
+    g_resid, all_r, block_out, m_sum = call(
+        backward_kernel,
+        4,
+        "backward_exchange",
+        args,
+        [HBM, HBM, VMEM, VMEM, HBM],
+        outs,
+        [VMEM, HBM, HBM, VMEM],
+        scratch,
+    )
+    return g_resid, all_r.reshape(ROWS, D), block_out.reshape(2 * HALF, D), m_sum
+
+
+def key_grads_kernel(*refs):
+    ins, outs, buffers, sems, deal = split(refs, 2, 2, 2, 3, 3)
+    p_ref, m_ref = ins
+    out_ref, dealt = outs
+    mine, land = buffers
+    lsem, send, recv = sems
+    greet(members()[1:] + across()[1:])
+    x = lax.axis_index("x")
+    own = pltpu.make_async_copy(p_ref.at[x], mine, lsem)
     own.start()
     copies = []
-    for i, s in enumerate(moves):
-        c = remote(p_ref.at[place(("x",), s)], land.at[i], send.at[i], recv.at[i], peer(("x",), s))
+    for i, s in enumerate(TURNS):
+        c = remote(
+            p_ref.at[place(("x",), (s,))], land.at[i], send.at[i], recv.at[i], peer(("x",), (s,))
+        )
         c.start()
         copies.append(c)
+    deals = deal_start(m_ref, dealt, deal)
     own.wait()
     out_ref[...] = mine[...].astype(F32)
     for i in range(3):
         copies[i].wait()
         out_ref[...] += land[i].astype(F32)
-
-
-def scatter_x(p):
-    dma = pltpu.SemaphoreType.DMA
-    wide = p.shape[1]
-    return pl.pallas_call(
-        scatter_x_kernel,
-        out_shape=jax.ShapeDtypeStruct((ROWS, wide), F32),
-        in_specs=[pl.BlockSpec(memory_space=pl.ANY)],
-        out_specs=pl.BlockSpec(memory_space=pltpu.VMEM),
-        scratch_shapes=[
-            pltpu.VMEM((ROWS, wide), BF),
-            pltpu.VMEM((3, ROWS, wide), BF),
-            dma,
-            dma((3,)),
-            dma((3,)),
-        ],
-        compiler_params=pltpu.CompilerParams(collective_id=5, has_side_effects=True),
-        cost_estimate=pl.CostEstimate(flops=0, bytes_accessed=30_000_000, transcendentals=0),
-        name="scatter_key_grads",
-    )(p.reshape(4, ROWS, wide))
+    finish(deals)
+
+
+def exchange_key_grads(p, m_sum):
+    outs = [((ROWS, 128), F32), ((MEMBERS, 32, 1536), BF)]
+    scratch = [pltpu.VMEM((ROWS, 128), BF), pltpu.VMEM((3, ROWS, 128), BF)]
+    scratch += [DMA, DMA((3,)), DMA((3,))] + DEAL_SEMS
+    args = (p.reshape(4, ROWS, 128), m_sum.reshape(MEMBERS, 32, 1536))
+    return call(
+        key_grads_kernel, 5, "exchange_key_grads", args, [HBM] * 2, outs, [VMEM, HBM], scratch
+    )
+
+
+def last_kernel(*refs):
+    ins, outs, slots_a, slots_c, others, sems_a, sems_c, deal, osems = split(
+        refs, 4, 2, 4, 4, 3, 5, 3, 3, 3
+    )
+    p_ref, rows_ref, g_resid, ag_ref = ins
+    input_grad, dealt = outs
+    total, grad, a_sum = others
+    greet(members() + across())
+    t = lax.axis_index("t")
+    state_a = scatter_start(p_ref, slots_a, sems_a)
+    state_c = reduce_start(ag_ref, slots_c, sems_c)
+    sent_a = scatter_send(state_a, slots_a, sems_a)
+    reduce_pass(state_c, slots_c, sems_c)
+    scatter_total(state_a, sent_a, slots_a, total)
+    rows = rows_ref[...]
+    inverse = scale_rows(rows)
+    grad[...] = g_resid[...] + norm_back(rows * inverse, inverse, total[...])
+    osend, orecv, local = osems
+    copies = [
+        pltpu.make_async_copy(grad, input_grad.at[t], local),
+        remote(grad, input_grad.at[t], osend, orecv, other_core()),
+    ]
+    for c in copies:
+        c.start()
+    reduce_total(state_c, slots_c, a_sum)
+    finish(deal_start(a_sum.reshape(MEMBERS, 32, 384), dealt, deal) + copies)
+
+
+def last_exchange(p, rows, g_resid, grads):
+    slots = (MEMBERS, 2, HALF, D)
+    outs = [((2, HALF, D), F32), ((MEMBERS, 32, 384), BF)]
+    scratch = scatter_slots(D) + reduce_slots(384)
+    scratch += [pltpu.VMEM((HALF, D), F32), pltpu.VMEM((HALF, D), F32), pltpu.VMEM((256, 384), BF)]
+    scratch += SCATTER_SEMS + REDUCE_SEMS + DEAL_SEMS + [DMA, DMA, DMA]
+    args = (p.reshape(slots), rows, g_resid, grads.reshape(2, 4, 256, 384))
+    input_grad, dealt = call(
+        last_kernel, 6, "last_exchange", args, [HBM, VMEM, VMEM, HBM], outs, [HBM, HBM], scratch
+    )
+    return input_grad.reshape(2 * HALF, D), dealt
 
 
 def abt(left, right):
@@ -436,54 +761,8 @@
     )(lo, hi, q, g, kv, kvt, row, start, lse, row_dot)
 
 
-def permute(x, axes, shift):
-    count = math.prod(SIZES[a] for a in axes)
-    pairs = []
-    for source, at in enumerate(shifts(axes)):
-        target = 0
-        for a, c, s in zip(axes, at, shift):
-            target = target * SIZES[a] + (c + s) % SIZES[a]
-        pairs.append((source, target))
-    assert len(pairs) == count
-    return lax.ppermute(x, axes, pairs)
-
-
 def swap_cores(x):
     return lax.ppermute(x, "t", [(0, 1), (1, 0)])
-
-
-def gather_over(x, axes):
-    moves = shifts(axes)
-    out = jnp.zeros((len(moves),) + x.shape, x.dtype)
-    out = lax.dynamic_update_index_in_dim(out, x, place(axes, moves[0]), 0)
-    for s in moves[1:]:
-        out = lax.dynamic_update_index_in_dim(out, permute(x, axes, s), place(axes, s, -1), 0)
-    return out
-
-
-def sum_over(x, axes):
-    moves = shifts(axes)
-    total = lax.dynamic_index_in_dim(x, place(axes, moves[0]), 0, keepdims=False).astype(F32)
-    for s in moves[1:]:
-        chunk = lax.dynamic_index_in_dim(x, place(axes, s), 0, keepdims=False)
-        total = total + permute(chunk, axes, s).astype(F32)
-    return total
-
-
-def deal(x):
-    return lax.all_to_all(x, GROUP, split_axis=0, concat_axis=0, tiled=True)
-
-
-def spread(weight_slots):
-    dealt = deal(weight_slots)
-    wide = weight_slots.shape[2]
-    return gather_over(dealt.reshape(MEMBERS * 32, wide), CROSS).reshape(D, wide)
-
-
-def collect(gradient):
-    wide = gradient.shape[1]
-    own = sum_over(gradient.reshape(8, 256, wide), CROSS)
-    return deal(own.astype(BF).reshape(MEMBERS, 32, wide)).astype(F32)
 
 
 def rope_frequency():
@@ -565,32 +844,25 @@
     low = lambda w: w.astype(BF).astype(F32)
     fold = lambda g, w: (g * low(w)).astype(BF)
     twice = lambda w: jnp.repeat(slots(w, HEAD_DIM), 2, axis=0)
-    attn_slots = jnp.concatenate(
+    qkv_slots = jnp.concatenate(
         [
             slots(fold(gain_a, query_weight), 128),
             twice(fold(gain_a, key_weight)),
             twice(fold(gain_a, value_weight)),
-            slots(output_weight.astype(BF).T, 128),
         ],
         axis=2,
     )
-    mlp_slots = jnp.concatenate(
-        [
-            slots(fold(gain_m, gate_weight), 512),
-            slots(fold(gain_m, up_weight), 512),
-            slots(down_weight.astype(BF).T, 512),
-        ],
-        axis=2,
-    )
-    attn_w = spread(attn_slots)
-    mlp_w = spread(mlp_slots)
-    w_qkv, w_out = attn_w[:, :256], attn_w[:, 256:]
-    w_gate_up, w_down = mlp_w[:, :1024], mlp_w[:, 1024:]
+    out_slots = slots(output_weight.astype(BF).T, 128)
+    gate_up_slots = jnp.concatenate(
+        [slots(fold(gain_m, gate_weight), 512), slots(fold(gain_m, up_weight), 512)], axis=2
+    )
+    down_slots = slots(down_weight.astype(BF).T, 512)
 
     rows = lax.dynamic_slice_in_dim(tokens[0], t * HALF, HALF, 0).astype(F32)
-    inv_a = lax.rsqrt(jnp.mean(rows * rows, axis=1, keepdims=True) + EPS)
-    unit_a = rows * inv_a
-    all_a, seg = gather_tokens(unit_a.astype(BF), jnp.broadcast_to(segments, (8, 128)))
+    unit_a = rows * scale_rows(rows)
+    all_a, seg, w_qkv, w_out = first_exchange(
+        unit_a.astype(BF), jnp.broadcast_to(segments, (8, 128)), qkv_slots, out_slots
+    )
     segment = seg[:, :, 0, :].reshape(LENGTH)
     index = jnp.arange(LENGTH, dtype=jnp.int32)
     previous = jnp.concatenate([jnp.full((1,), -1, jnp.int32), segment[:-1]])
@@ -608,7 +880,7 @@
     qkv = jnp.dot(all_a, w_qkv, preferred_element_type=F32)
     rotated = rotate(qkv[:, :192], cos_tab, sin_tab).astype(BF)
     kv_own = jnp.concatenate([rotated[:, 128:], qkv[:, 192:].astype(BF)], axis=1)
-    kv = gather_x(kv_own)
+    kv, gate_up_part, down_part = exchange_keys(kv_own, gate_up_slots, down_slots)
     kvt = kv.T
     scale = HEAD_DIM ** (-0.5)
     q_low = heads_apart(rotated[:, :128])
@@ -618,47 +890,28 @@
     o_full = heads_beside(o_cols[:, HEAD_DIM:])
     o_low = o_full.astype(BF)
 
-    resid = rows + scatter_sum(abt(o_low, w_out).astype(BF))
-    inv_m = lax.rsqrt(jnp.mean(resid * resid, axis=1, keepdims=True) + EPS)
-    unit_m = resid * inv_m
-    all_m = gather_tokens(unit_m.astype(BF))
+    cot_half = lax.dynamic_slice_in_dim(cotangent[0], t * HALF, HALF, 0)
+    resid, all_m, all_g, w_gate_up, w_down = forward_exchange(
+        abt(o_low, w_out).astype(BF), rows, cot_half, gate_up_part, down_part
+    )
     gate_up = jnp.dot(all_m, w_gate_up, preferred_element_type=F32)
     gate, up = gate_up[:, :512], gate_up[:, 512:]
     sig = jax.nn.sigmoid(gate)
     silu = gate * sig
     act = (silu * up).astype(BF)
 
-    cot_half = lax.dynamic_slice_in_dim(cotangent[0], t * HALF, HALF, 0)
-    cot_own = gather_over(cot_half, GROUP)
-    cot_other = swap_cores(cot_own)
-    all_g = jnp.where(
-        t == 0, jnp.stack([cot_own, cot_other], axis=1), jnp.stack([cot_other, cot_own], axis=1)
-    ).reshape(ROWS, D)
-
     g_act = jnp.dot(all_g, w_down, preferred_element_type=F32)
     g_gate = g_act * up * sig * (1.0 + gate * (1.0 - sig))
     g_up = g_act * silu
     g_gate_up = jnp.concatenate([g_gate, g_up], axis=1).astype(BF)
-    g_unit_m = scatter_sum(abt(g_gate_up, w_gate_up).astype(BF))
-    grad_out = cot_half.astype(F32)
-    g_resid = grad_out + inv_m * (
-        g_unit_m - unit_m * jnp.mean(g_unit_m * unit_m, axis=1, keepdims=True)
-    )
-    all_r = gather_tokens(g_resid.astype(BF))
-
     mlp_grad = jnp.concatenate([atb(all_m, g_gate_up), atb(all_g, act)], axis=1).astype(BF)
-    mlp_sum = collect(mlp_grad)
-
-    down = abt(act, w_down).astype(BF).reshape(MEMBERS, 2, HALF, D)
-    pick = lambda v, i: lax.dynamic_index_in_dim(v, i, 1, keepdims=False)
-    down_pair = pick(down, t).astype(F32) + swap_cores(pick(down, 1 - t)).astype(F32)
-    out_half = (resid + sum_over(down_pair.astype(BF), GROUP)).astype(BF)
-    halves = lambda own: jnp.where(
-        t == 0,
-        jnp.concatenate([own, swap_cores(own)], axis=0),
-        jnp.concatenate([swap_cores(own), own], axis=0),
-    )
-    block_out = halves(out_half)
+    g_resid, all_r, block_out, mlp_part = backward_exchange(
+        abt(g_gate_up, w_gate_up).astype(BF),
+        abt(act, w_down).astype(BF),
+        resid,
+        cot_half,
+        mlp_grad,
+    )
 
     g_o = jnp.dot(all_r, w_out, preferred_element_type=F32).astype(BF)
     row_dot = (
@@ -672,17 +925,15 @@
     dq_cols, dkv = attend_back(
         lo, hi, q_wide, g_wide, kv, kvt, row_ids, row_starts, lse, row_dot
     )
-    g_kv = scatter_x(dkv)
+    g_kv, mlp_dealt = exchange_key_grads(dkv, mlp_part)
     g_q = heads_beside(dq_cols[:, :HEAD_DIM]) * scale
     g_turned = rotate(jnp.concatenate([g_q, g_kv[:, :HEAD_DIM]], axis=1), cos_tab, -sin_tab)
     g_qkv = jnp.concatenate([g_turned, g_kv[:, HEAD_DIM:]], axis=1).astype(BF)
     attn_grad = jnp.concatenate([atb(all_a, g_qkv), atb(all_r, o_low)], axis=1).astype(BF)
-    attn_sum = collect(attn_grad)
-    g_unit_a = scatter_sum(abt(g_qkv, w_qkv).astype(BF))
-    input_half = g_resid + inv_a * (
-        g_unit_a - unit_a * jnp.mean(g_unit_a * unit_a, axis=1, keepdims=True)
-    )
-    input_grad = halves(input_half)
+    input_grad, attn_dealt = last_exchange(
+        abt(g_qkv, w_qkv).astype(BF), rows, g_resid, attn_grad
+    )
+    mlp_sum, attn_sum = mlp_dealt.astype(F32), attn_dealt.astype(F32)
 
     pairs = lambda g: unslots(g.reshape(4, 2, 32, HEAD_DIM).sum(axis=1))
     q_sum = unslots(attn_sum[:, :, :128])

time: 709 us -> 503 us (0.71)
  waiting for transfers between devices: 142 us -> 0.01 us
  starting transfers between devices: 119 us -> 1.26 us
  Pallas kernels: 261 us -> 347 us
  local copies, waits for them, and re-layouts: 94.1 us -> 59.6 us
  matrix products: 42.3 us -> 56 us
  other arithmetic: 39.7 us -> 31.5 us
    pallas_call x8 -> x6, Pallas kernels: 250 us -> 335 us  [call(): pl.pallas_call(kernel, out_shape=[jax.ShapeDtypeStruct(s, d) for s, d in...]
    ppermute x42 -> x0, starting transfers between devices: 77.9 us -> none  [permute(): return lax.ppermute(x, axes, pairs)]
    ppermute x42 -> x0, waiting for transfers between devices: 73.9 us -> none  [permute(): return lax.ppermute(x, axes, pairs)]
    all_to_all x4 -> x0, waiting for transfers between devices: 67.8 us -> none  [deal(): return lax.all_to_all(x, GROUP, split_axis=0, concat_axis=0, tiled=True)]
    ppermute x5 -> x1, starting transfers between devices: 24.9 us -> 1.26 us  [swap_cores(): return lax.ppermute(x, 't', [(0, 1), (1, 0)])]
    all_to_all x4 -> x0, starting transfers between devices: 16 us -> none  [deal(): return lax.all_to_all(x, GROUP, split_axis=0, concat_axis=0, tiled=True)]
    dynamic_update_slice x23 -> x0, local copies, waits for them, and re-layouts: 14.1 us -> none  [the longest x21 12.8 us: gather_over(): lax.dynamic_update_index_in_dim(out, permute(x, axes, s), place(axes, s,...]
    unnamed x173 -> x109, local copies, waits for them, and re-layouts: 15.7 us -> 6.15 us
  transfers between devices with their start and end apart: 51 -> 1, of which waited for: 8 -> 0; matrix products, arithmetic and copies ran while one was open for 16% -> 0% of each run, Pallas kernels for 24% -> 0%
where the time goes in v2:
time: 503 us; the launch traced here: 497 us
  Pallas kernels  347 us (69%)
  local copies, waits for them, and re-layouts  59.6 us (12%)
  matrix products  56 us (11%)
  other arithmetic  31.5 us (6%)
    pallas_call x6, Pallas kernels, call(): pl.pallas_call(kernel, out_shape=[jax.ShapeDtypeStruct(s, d) for s, d in...  335 us
    dot_general x4, local copies, waits for them, and re-layouts, atb(): lax.dot_general(left, right, (((0,), (0,)), ((), ())), preferred_element_...  26.3 us
    dot_general x4, matrix products, abt(): lax.dot_general(left, right, (((1,), (1,)), ((), ())), preferred_element_...  20.2 us
    dot_general x4, matrix products, atb(): lax.dot_general(left, right, (((0,), (0,)), ((), ())), preferred_element_...  15.6 us
  transfers between devices with their start and end apart: 1, of which 0 were waited for; matrix products, arithmetic and copies ran while one was open for 0% of the time, Pallas kernels for 0%

profile of v2, /device:TPU:1, one launch (start us, length us, event | category | flops | bytes accessed | tf_op | source)
XLA Modules:
  0.0 497.4 jit_solution(17709464288636761004)
XLA Ops:
  9.9 48.1 %first_exchange.1 = (bf16[8,2,64,2048]{3,2,1,0:T(8,128)(2,1)}, s32[4,8,8,128]{3,2,1,0:T(8,128)}, bf16[2,4,8,32,256]{4,3,2,1,0:T(8,128)(2,1)}, bf16[2,4,8,32,128]{4,3,2,1,0:T(8,128)(2,1)}) custom-call(bf16[64,2048]{1,0:T(8,128)(2,1)} %multiply_convert_fusion.3.refs_0_, s32[8,128]{1,0:T(8,128)} %broadcast_in_dim.13.refs_1_, ...), custom_call_target="tpu_custom_call" | custom-call | bytes 60000000 | tf_op jit(solution)/shard_map/first_exchange/pallas_call | solution.py:331
  58.0 3.8 fusion.40
  68.5 13.3 %exchange_keys.1 = (bf16[4,1024,128]{2,1,0:T(8,128)(2,1)}, bf16[8,32,1024]{2,1,0:T(8,128)(2,1)}, bf16[8,32,512]{2,1,0:T(8,128)(2,1)}) custom-call(bf16[1024,128]{1,0:T(8,128)(2,1)} %pad_maximum_fusion.12.refs_0_, bf16[8,32,1024]{2,1,0:T(8,128)(2,1)} %pad_maximum_fusion.6.refs_1_, bf16[8,32,512]{2,1,0:T(8,128)(2,1)} %bitcast.250), custom_call_target="tpu_custom_call" | custom-call | bytes 60000000 | tf_op jit(solution)/shard_map/exchange_keys/pallas_call | solution.py:331
  84.5 5.3 %attend.1 = (f32[4,128,512]{2,1,0:T(8,128)S(1)}, f32[4,1,512]{2,1,0:T(1,128)S(1)}) custom-call(s32[4]{0:T(128)S(1)} %get-tuple-element.156.lo_ref, s32[4]{0:T(128)S(1)} %get-tuple-element.155.hi_ref, bf16[4,512,128]{2,1,0:T(8,128)(2,1)S(1)} %concatenate.50.q_ref, bf16[4096,128]{1,0:T(8,128)(2,1)S(1)} %bitcast.202, bf16[128,4096]{1,0:T(8,128)(2,1)S(1)} %bitcast.204, ...), custom_call_target="tpu_custom_call" | custom-call | flops 2000000000 | bytes 60000000 | tf_op jit(solution)/shard_map/attend/pallas_call | solution.py:709
  96.3 4.3 convolution_convert_fusion.2
  100.7 103.5 %forward_exchange.1 = (f32[64,2048]{1,0:T(8,128)}, bf16[8,2,64,2048]{3,2,1,0:T(8,128)(2,1)}, bf16[8,2,64,2048]{3,2,1,0:T(8,128)(2,1)}, bf16[2,4,8,32,1024]{4,3,2,1,0:T(8,128)(2,1)}, bf16[2,4,8,32,512]{4,3,2,1,0:T(8,128)(2,1)}) custom-call(bf16[8,2,64,2048]{3,2,1,0:T(8,128)(2,1)} %bitcast.209, f32[64,2048]{1,0:T(8,128)} %get-tuple-element.157.refs_1_, ...), custom_call_target="tpu_custom_call" | custom-call | bytes 60000000 | tf_op jit(solution)/shard_map/forward_exchange/pallas_call | solution.py:331
  204.2 6.4 %copy.199 = bf16[2048,1024]{1,0:T(8,128)(2,1)} copy(bf16[2048,1024]{0,1:T(8,128)(2,1)} %bitcast.216) | data formatting | bytes 8388608 | tf_op jit(solution)/shard_map/dot_general | solution.py:627
  210.6 8.0 %fusion.41 = f32[1024,1024]{0,1:T(8,128)S(1)} fusion(bf16[1024,2048]{1,0:T(8,128)(2,1)} %bitcast.217, bf16[2048,1024]{1,0:T(8,128)(2,1)} %bitcast.266), kind=kOutput, calls=%fused_computation.149 | convolution fusion | flops 4294967296 | bytes 12582912 | tf_op jit(solution)/shard_map/dot_general | solution.py:897
  218.6 4.1 multiply_convert_fusion.2
  222.7 6.1 %convolution_convert_fusion.3 = bf16[1024,2048]{1,0:T(8,128)(2,1)} fusion(bf16[2048,1024]{1,0:T(8,128)(2,1)S(1)} %bitcast.267, bf16[1024,512]{0,1:T(8,128)(2,1)S(1)} %get-tuple-element.118, bf16[1024,512]{0,1:T(8,128)(2,1)S(1)} %get-tuple-element.117), kind=kOutput, calls=%fused_computation.4 | convolution fusion | flops 4301258752 | bytes 10485760 | tf_op jit(solution)/shard_map/dot_general | solution.py:623
  228.8 7.0 %convolution_convert_fusion.4 = bf16[2,4,256,1024]{3,2,1,0:T(8,128)(2,1)} fusion(bf16[2,4,256,1024]{3,2,1,0:T(8,128)(2,1)S(1)} %bitcast.218, bf16[1024,512]{0,1:T(8,128)(2,1)S(1)} %get-tuple-element.118, bf16[1024,512]{0,1:T(8,128)(2,1)S(1)} %get-tuple-element.117), kind=kOutput, calls=%fused_computation.5 | convolution fusion | flops 4301258752 | bytes 10485760 | tf_op jit(solution)/shard_map/dot_general | solution.py:627
  235.9 6.8 %copy.201 = bf16[2048,1024]{1,0:T(8,128)(2,1)} copy(bf16[2048,1024]{0,1:T(8,128)(2,1)} %bitcast.213) | data formatting | bytes 8388608 | tf_op jit(solution)/shard_map/dot_general | solution.py:627
  242.7 6.5 %convolution_convert_fusion.1 = bf16[1024,2048]{1,0:T(8,128)(2,1)} fusion(bf16[1024,512]{0,1:T(8,128)(2,1)} %get-tuple-element.119, bf16[2048,512]{1,0:T(8,128)(2,1)} %bitcast.268), kind=kOutput, calls=%fused_computation.2 | convolution fusion | flops 2149580800 | bytes 7340032 | tf_op jit(solution)/shard_map/dot_general | solution.py:623
  249.2 3.9 convolution_convert_fusion.5
  255.2 6.1 %pad_maximum_fusion.refs_4_ = bf16[2,4,256,1536]{3,2,1,0:T(8,128)(2,1)} fusion(bf16[2,4,256,512]{3,2,1,0:T(8,128)(2,1)} %convolution_convert_fusion.5, bf16[2,4,256,1024]{3,2,1,0:T(8,128)(2,1)} %convolution_convert_fusion.4), kind=kLoop, calls=%fused_computation | loop fusion | flops 12582912 | bytes 12582912 | tf_op jit(solution)/shard_map/concatenate | solution.py:907
  261.2 98.2 %backward_exchange.1 = (f32[64,2048]{1,0:T(8,128)}, bf16[8,2,64,2048]{3,2,1,0:T(8,128)(2,1)}, bf16[2,64,2048]{2,1,0:T(8,128)(2,1)}, bf16[256,1536]{1,0:T(8,128)(2,1)}) custom-call(bf16[8,2,64,2048]{3,2,1,0:T(8,128)(2,1)} %bitcast.220, bf16[8,2,64,2048]{3,2,1,0:T(8,128)(2,1)} %bitcast.221, f32[64,2048]{1,0:T(8,128)} %get-tuple-element.70.refs_2_, ...), custom_call_target="tpu_custom_call" | custom-call | bytes 60000000 | tf_op jit(solution)/shard_map/backward_exchange/pallas_call | solution.py:331
  359.4 4.2 convert_multiply_fusion.4
  371.6 7.1 %attend_back.1 = (f32[4,128,512]{2,1,0:T(8,128)S(1)}, bf16[4096,128]{1,0:T(8,128)(2,1)S(1)}) custom-call(s32[4]{0:T(128)S(1)} %get-tuple-element.156.lo_ref, s32[4]{0:T(128)S(1)} %get-tuple-element.155.hi_ref, bf16[4,512,128]{2,1,0:T(8,128)(2,1)S(1)} %concatenate.50.q_ref, bf16[4,512,128]{2,1,0:T(8,128)(2,1)S(1)} %concatenate.57.g_ref, ...), custom_call_target="tpu_custom_call" | custom-call | flops 5000000000 | bytes 120000000 | tf_op jit(solution)/shard_map/attend_back/pallas_call | solution.py:735
  380.5 30.5 %exchange_key_grads.1 = (f32[1024,128]{1,0:T(8,128)}, bf16[8,32,1536]{2,1,0:T(8,128)(2,1)}) custom-call(bf16[4,1024,128]{2,1,0:T(8,128)(2,1)} %bitcast.200, bf16[8,32,1536]{2,1,0:T(8,128)(2,1)} %bitcast.253), custom_call_target="tpu_custom_call" | custom-call | bytes 60000000 | tf_op jit(solution)/shard_map/exchange_key_grads/pallas_call | solution.py:331
  413.5 6.5 %copy.212 = bf16[2048,1024]{1,0:T(8,128)(2,1)} copy(bf16[2048,1024]{0,1:T(8,128)(2,1)} %bitcast.212) | data formatting | bytes 8388608 | tf_op jit(solution)/shard_map/dot_general | solution.py:627
  420.3 3.3 convolution_convert_fusion
  424.9 6.5 %copy.214 = bf16[2048,1024]{1,0:T(8,128)(2,1)} copy(bf16[2048,1024]{0,1:T(8,128)(2,1)} %bitcast.208) | data formatting | bytes 8388608 | tf_op jit(solution)/shard_map/dot_general | solution.py:627
  431.5 3.4 convolution_convert_fusion.7
  436.3 41.3 %last_exchange.1 = (f32[2,64,2048]{2,1,0:T(8,128)}, bf16[8,32,384]{2,1,0:T(8,128)(2,1)}) custom-call(bf16[8,2,64,2048]{3,2,1,0:T(8,128)(2,1)} %bitcast.206, f32[64,2048]{1,0:T(8,128)} %get-tuple-element.157.refs_1_, f32[64,2048]{1,0:T(8,128)} %get-tuple-element.78.refs_2_, bf16[2,4,256,384]{3,2,1,0:T(8,128)(2,1)} %pad_maximum_fusion.2.refs_3_), custom_call_target="tpu_custom_call" | custom-call | bytes 60000000 | tf_op jit(solution)/shard_map/last_exchange/pallas_call | solution.py:331
  (204 shorter events, 61.3 us)
Async XLA Ops:
  210.6 8.0 %copy-start.2 = (bf16[8,2,64,2048]{3,2,1,0:T(8,128)(2,1)S(1)}, bf16[8,2,64,2048]{3,2,1,0:T(8,128)(2,1)}, u32[]{:S(2)}) copy-start(bf16[8,2,64,2048]{3,2,1,0:T(8,128)(2,1)} %get-tuple-element.66) | copy-start | bytes 12582916
  210.6 8.0 %copy-start.48 = (bf16[2,4,8,32,512]{4,3,2,1,0:T(8,128)(2,1)S(1)}, bf16[2,4,8,32,512]{4,3,2,1,0:T(8,128)(2,1)}, u32[]{:S(2)}) copy-start(bf16[2,4,8,32,512]{4,3,2,1,0:T(8,128)(2,1)} %get-tuple-element.67) | copy-start | bytes 6291460
  222.7 6.1 %copy-start.4 = (bf16[2048,1024]{1,0:T(8,128)(2,1)S(1)}, bf16[2048,1024]{1,0:T(8,128)(2,1)}, u32[]{:S(2)}) copy-start(bf16[2048,1024]{1,0:T(8,128)(2,1)} %copy.199) | copy-start | bytes 12582916
  242.7 6.5 %copy-start.5 = (bf16[2048,1024]{1,0:T(8,128)(2,1)S(1)}, bf16[2048,1024]{1,0:T(8,128)(2,1)}, u32[]{:S(2)}) copy-start(bf16[2048,1024]{1,0:T(8,128)(2,1)} %copy.201) | copy-start | bytes 12582916
  242.7 6.5 %copy-start.49 = (bf16[1024,512]{0,1:T(8,128)(2,1)S(1)}, bf16[1024,512]{0,1:T(8,128)(2,1)}, u32[]{:S(2)}) copy-start(bf16[1024,512]{0,1:T(8,128)(2,1)} %get-tuple-element.119) | copy-start | bytes 3145732
  261.2 98.2 %copy-start.6 = (bf16[2,4,8,32,128]{4,3,2,1,0:T(8,128)(2,1)S(1)}, bf16[2,4,8,32,128]{4,3,2,1,0:T(8,128)(2,1)}, u32[]{:S(2)}) copy-start(bf16[2,4,8,32,128]{4,3,2,1,0:T(8,128)(2,1)} %get-tuple-element.63) | copy-start | bytes 1572868
  413.5 6.6 %copy-start.16 = (f32[1024,32]{0,1:T(8,128)S(1)}, f32[1024,32]{0,1:T(8,128)}, u32[]{:S(2)}) copy-start(f32[1024,32]{0,1:T(8,128)} %copy-done.15) | copy-start | bytes 393220
  413.5 6.6 %copy-start.30 = (f32[1024,32]{0,1:T(8,128)S(1)}, f32[1024,32]{0,1:T(8,128)}, u32[]{:S(2)}) copy-start(f32[1024,32]{0,1:T(8,128)} %get-tuple-element.134) | copy-start | bytes 393220
  413.5 6.8 %copy-start.17 = (bf16[2,4,8,32,256]{4,3,2,1,0:T(8,128)(2,1)S(1)}, bf16[2,4,8,32,256]{4,3,2,1,0:T(8,128)(2,1)}, u32[]{:S(2)}) copy-start(bf16[2,4,8,32,256]{4,3,2,1,0:T(8,128)(2,1)} %get-tuple-element.60) | copy-start | bytes 3145732
  424.9 6.6 %copy-start.18 = (bf16[1024,128,1,1]{0,1,2,3:T(8,128)(2,1)S(1)}, bf16[1024,128,1,1]{0,1,2,3:T(8,128)(2,1)}, u32[]{:S(2)}) copy-start(bf16[1024,128,1,1]{0,1,2,3:T(8,128)(2,1)} %reshape.442) | copy-start | bytes 786436
  436.3 49.0 %copy-start.20 = (bf16[8,32,1536]{2,1,0:T(8,128)(2,1)S(1)}, bf16[8,32,1536]{2,1,0:T(8,128)(2,1)}, u32[]{:S(2)}) copy-start(bf16[8,32,1536]{2,1,0:T(8,128)(2,1)} %get-tuple-element.81) | copy-start | bytes 2359300
  479.3 6.4 %copy-start.8 = (f32[32,4096]{1,0:T(8,128)S(1)}, f32[32,4096]{1,0:T(8,128)}, u32[]{:S(2)}) copy-start(f32[32,4096]{1,0:T(8,128)} %param.34) | copy-start | bytes 1572868
  479.3 6.4 %copy-start.10 = (f32[32,4096]{1,0:T(8,128)S(1)}, f32[32,4096]{1,0:T(8,128)}, u32[]{:S(2)}) copy-start(f32[32,4096]{1,0:T(8,128)} %param.35) | copy-start | bytes 1572868
  479.3 6.4 %copy-start.21 = (f32[32,4096]{1,0:T(8,128)S(1)}, f32[32,4096]{1,0:T(8,128)}, u32[]{:S(2)}) copy-start(f32[32,4096]{1,0:T(8,128)} %param.50) | copy-start | bytes 1572868
  479.3 6.4 %copy-start.22 = (f32[32,4096]{1,0:T(8,128)S(1)}, f32[32,4096]{1,0:T(8,128)}, u32[]{:S(2)}) copy-start(f32[32,4096]{1,0:T(8,128)} %param.42) | copy-start | bytes 1572868
  479.3 6.5 %copy-start.23 = (f32[32,4096]{1,0:T(8,128)S(1)}, f32[32,4096]{1,0:T(8,128)}, u32[]{:S(2)}) copy-start(f32[32,4096]{1,0:T(8,128)} %param.51) | copy-start | bytes 1572868
  486.4 6.0 %copy-start.29 = (f32[1024,32]{0,1:T(8,128)S(1)}, f32[1024,32]{0,1:T(8,128)}, u32[]{:S(2)}) copy-start(f32[1024,32]{0,1:T(8,128)} %param.33) | copy-start | bytes 393220
  486.4 6.0 %copy-start.31 = (f32[8,4,8,128]{3,2,1,0:T(8,128)S(1)}, f32[8,4,8,128]{3,2,1,0:T(8,128)}, u32[]{:S(2)}) copy-start(f32[8,4,8,128]{3,2,1,0:T(8,128)} %get-tuple-element.129) | copy-start | bytes 393220
  486.5 6.9 %copy-start.12 = (f32[4096,32]{0,1:T(8,128)S(1)}, f32[4096,32]{0,1:T(8,128)}, u32[]{:S(2)}) copy-start(f32[4096,32]{0,1:T(8,128)} %param.36) | copy-start | bytes 1572868
  486.5 6.9 %copy-start.25 = (f32[4096,32]{0,1:T(8,128)S(1)}, f32[4096,32]{0,1:T(8,128)}, u32[]{:S(2)}) copy-start(f32[4096,32]{0,1:T(8,128)} %param.52) | copy-start | bytes 1572868
  486.5 6.9 %copy-start.26 = (f32[4096,32]{0,1:T(8,128)S(1)}, f32[4096,32]{0,1:T(8,128)}, u32[]{:S(2)}) copy-start(f32[4096,32]{0,1:T(8,128)} %param.44) | copy-start | bytes 1572868
  489.0 6.4 %copy-start.28 = (bf16[2,64,2048]{2,1,0:T(8,128)(2,1)S(1)}, bf16[2,64,2048]{2,1,0:T(8,128)(2,1)}, u32[]{:S(2)}) copy-start(bf16[2,64,2048]{2,1,0:T(8,128)(2,1)} %get-tuple-element.71) | copy-start | bytes 1572868
  489.1 7.1 %copy-start.19 = (f32[2,64,2048]{2,1,0:T(8,128)S(1)}, f32[2,64,2048]{2,1,0:T(8,128)}, u32[]{:S(2)}) copy-start(f32[2,64,2048]{2,1,0:T(8,128)} %get-tuple-element.79) | copy-start | bytes 3145732
  491.1 3.7 collective-permute-start
  (27 other events, 104.6 us)
